TPU v7x, 256 devices: a whole 4x4x8 slice. The times are simulated.
256 devices in a mesh: pen: 32 (over y, z_lo, core), chan: 8 (over x, z_hi).
Axes of the slice: x: 4, y: 4, z: 8 (z_hi: 2, z_lo: 4; z = z_hi * 4 + z_lo), core: 2. Of those that a mesh axis runs over, the one named last changes fastest.
Arguments:
- latents: bfloat16 [384, 1440, 256], P('pen', 'chan'), may hold values from -6 to 6
- norm_gain: float32 [256], replicated, may hold values from 0.1 to 1.9
- weight_in: bfloat16 [1024, 256], P(('pen', 'chan')), may hold values from -0.375 to 0.375
- weight_out: bfloat16 [1024, 256], P(('pen', 'chan')), may hold values from -0.1875 to 0.1875
- filter_first: bfloat16 [2, 8, 32, 32], P(None, 'chan'), may hold values from -0.75 to 0.75
- filter_second: bfloat16 [2, 8, 32, 32], P(None, 'chan'), may hold values from -0.75 to 0.75
- cotangent: bfloat16 [384, 1440, 256], P('pen', 'chan'), may hold values from -6 to 6
Outputs:
- block_output: bfloat16 [384, 1440, 256], P('pen', 'chan')
- grad_latents: bfloat16 [384, 1440, 256], P('pen', 'chan')
- grad_weight_in: float32 [1024, 256], P(('pen', 'chan'))
- grad_weight_out: float32 [1024, 256], P(('pen', 'chan'))
- grad_filter_first: float32 [2, 8, 32, 32], P(None, 'chan')
- grad_filter_second: float32 [2, 8, 32, 32], P(None, 'chan')
All inputs are finite; a program needn't handle non-finite values.
Results may differ from a plain program's by a relative error of at most 0.015.
The roundings to bfloat16 on the way count: a program that leaves them out, or rounds other values in their place, can miss the bound.
Values may be sent and summed in bfloat16 or wider, within the bound.
A program may use at most 128 MiB of HBM per device.

v0:
```python
import math

import jax
import jax.numpy as jnp
from jax import lax
from jax.sharding import PartitionSpec as P

NLAT = 384
NLON = 1440
KLON = 384


def zonal_tables():
    column = jnp.arange(NLON, dtype=jnp.int32)[:, None]
    number = jnp.arange(KLON, dtype=jnp.int32)[None, :]
    phase = (column * number % NLON).astype(jnp.float32) * (2.0 * math.pi / NLON)
    factor = 1.0 / math.sqrt(NLON)
    forward = jnp.concatenate([jnp.cos(phase), -jnp.sin(phase)], axis=1) * factor
    weights = jnp.where(number == 0, 1.0, 2.0).astype(jnp.float32)
    inverse = (
        jnp.concatenate([jnp.cos(phase) * weights, -jnp.sin(phase) * weights], axis=1).T * factor
    )
    return (forward.astype(jnp.bfloat16), inverse.astype(jnp.bfloat16))


def meridian_table():
    row_mode = jnp.arange(NLAT, dtype=jnp.int32)[:, None]
    row_lat = jnp.arange(NLAT, dtype=jnp.int32)[None, :]
    phase = (row_mode * row_lat % NLAT).astype(jnp.float32) * (2.0 * math.pi / NLAT)
    factor = 1.0 / math.sqrt(NLAT)
    real_part = jnp.cos(phase) * factor
    imag_part = -jnp.sin(phase) * factor
    upper = jnp.stack([real_part, -imag_part], axis=1)
    lower = jnp.stack([imag_part, real_part], axis=1)
    return jnp.stack([upper, lower], axis=0).astype(jnp.bfloat16)


def normalize(values, norm_gain):
    centred = values - jnp.mean(values, axis=-1, keepdims=True)
    spread = jnp.mean(centred * centred, axis=-1, keepdims=True)
    return centred * lax.rsqrt(spread + 1e-05) * norm_gain


def complex_stack(matrix):
    return jnp.stack([jnp.stack([matrix[0], matrix[1]]), jnp.stack([-matrix[1], matrix[0]])])


def block_forward(spectra, first, second):
    first_act = jnp.einsum(
        "prba,pqbae->qrbe", spectra, complex_stack(first), preferred_element_type=jnp.float32
    )
    first_hidden = jax.nn.gelu(first_act).astype(jnp.bfloat16)
    second_act = jnp.einsum(
        "prba,pqbae->qrbe", first_hidden, complex_stack(second), preferred_element_type=jnp.float32
    )
    shrunk = (second_act - 0.1 * jnp.tanh(second_act * 10.0)).astype(jnp.bfloat16)
    return (shrunk, (first_act, first_hidden, second_act))


def fold_grad(outer):
    return jnp.stack([outer[0, 0] + outer[1, 1], outer[0, 1] - outer[1, 0]])


def block_backward(spectra, first, second, stored, d_shrunk):
    first_act, first_hidden, second_act = stored
    slope = jnp.tanh(second_act * 10.0)
    d_second = (d_shrunk.astype(jnp.float32) * slope * slope).astype(jnp.bfloat16)
    outer_two = jnp.einsum(
        "prba,qrbe->pqbae", first_hidden, d_second, preferred_element_type=jnp.float32
    )
    d_hidden = jnp.einsum(
        "qrbe,pqbae->prba", d_second, complex_stack(second), preferred_element_type=jnp.float32
    )
    unused, pull_gelu = jax.vjp(jax.nn.gelu, first_act)
    d_first = pull_gelu(d_hidden)[0].astype(jnp.bfloat16)
    outer_one = jnp.einsum("prba,qrbe->pqbae", spectra, d_first, preferred_element_type=jnp.float32)
    d_spectra = jnp.einsum(
        "qrbe,pqbae->prba", d_first, complex_stack(first), preferred_element_type=jnp.float32
    )
    return (d_spectra.astype(jnp.bfloat16), fold_grad(outer_one), fold_grad(outer_two))


def group_modes(modes):
    return modes.reshape(modes.shape[0], 2, lax.axis_size("pen"), -1)


def ungroup_modes(moved):
    return moved.reshape(moved.shape[0], 2, -1)


def to_meridional(modes):
    moved = lax.all_to_all(group_modes(modes), "pen", split_axis=2, concat_axis=0, tiled=True)
    return ungroup_modes(moved)


def to_zonal(spectra, band_width):
    grouped = spectra.reshape(spectra.shape[0], 2, 1, -1)
    moved = lax.all_to_all(grouped, "pen", split_axis=0, concat_axis=2, tiled=True)
    return moved.reshape(moved.shape[0], -1, band_width)


def to_column(spatial):
    return lax.all_to_all(spatial, "chan", split_axis=1, concat_axis=2, tiled=True)


def body(latents, norm_gain, weight_in, weight_out, filter_first, filter_second, cotangent):
    forward_zonal, inverse_zonal = zonal_tables()
    meridian = meridian_table()
    band_lat, band_lon, width = latents.shape
    block_count = filter_first.shape[1]
    block_size = filter_first.shape[2]
    band_width = block_count * block_size
    normed_f, pull_norm = jax.vjp(
        lambda values: normalize(values, norm_gain), latents.astype(jnp.float32)
    )
    normed = normed_f.astype(jnp.bfloat16)
    full_in, full_out = (
        lax.all_gather(weight_in, ("pen", "chan"), axis=0, tiled=True),
        lax.all_gather(weight_out, ("pen", "chan"), axis=0, tiled=True),
    )
    tokens = normed.reshape(-1, width)
    grad_tokens = cotangent.reshape(-1, width)
    pre_act = lax.dot_general(
        tokens, full_in, (((1,), (1,)), ((), ())), preferred_element_type=jnp.float32
    )
    hidden = jax.nn.gelu(pre_act).astype(jnp.bfloat16)
    column_mix = jnp.dot(hidden, full_out, preferred_element_type=jnp.float32)
    pencil_normed, pencil_grad = (
        lax.all_to_all(normed, "chan", split_axis=2, concat_axis=1, tiled=True),
        lax.all_to_all(cotangent, "chan", split_axis=2, concat_axis=1, tiled=True),
    )
    zonal_modes = jnp.einsum(
        "ljc,jq->lqc", pencil_normed, forward_zonal, preferred_element_type=jnp.float32
    ).astype(jnp.bfloat16)
    meridional_in = to_meridional(zonal_modes)
    lat_total = meridional_in.shape[0]
    spectrum = jnp.einsum(
        "qmpi,ipx->qmx", meridian, meridional_in, preferred_element_type=jnp.float32
    ).astype(jnp.bfloat16)
    blocks = spectrum.reshape(2, -1, block_count, block_size)
    shrunk, stored = block_forward(blocks, filter_first, filter_second)
    inverse_lat = jnp.einsum(
        "qmpi,qmx->ipx",
        meridian,
        shrunk.reshape(2, lat_total, -1),
        preferred_element_type=jnp.float32,
    ).astype(jnp.bfloat16)
    zonal_back = to_zonal(inverse_lat, band_width)
    spatial = jnp.einsum(
        "lqc,qj->ljc", zonal_back, inverse_zonal, preferred_element_type=jnp.float32
    ).astype(jnp.bfloat16)
    spectral_part = to_column(spatial)
    d_hidden = lax.dot_general(
        grad_tokens, full_out, (((1,), (1,)), ((), ())), preferred_element_type=jnp.float32
    )
    unused, pull_gelu = jax.vjp(jax.nn.gelu, pre_act)
    d_pre = pull_gelu(d_hidden)[0].astype(jnp.bfloat16)
    d_column = jnp.dot(d_pre, full_in, preferred_element_type=jnp.float32)
    term_in = lax.dot_general(
        d_pre, tokens, (((0,), (0,)), ((), ())), preferred_element_type=jnp.float32
    )
    term_out = lax.dot_general(
        hidden, grad_tokens, (((0,), (0,)), ((), ())), preferred_element_type=jnp.float32
    )
    grad_weight_in, grad_weight_out = (
        lax.psum_scatter(term_in, ("pen", "chan"), scatter_dimension=0, tiled=True),
        lax.psum_scatter(term_out, ("pen", "chan"), scatter_dimension=0, tiled=True),
    )
    d_inverse = jnp.einsum(
        "ljc,qj->lqc", pencil_grad, inverse_zonal, preferred_element_type=jnp.float32
    ).astype(jnp.bfloat16)
    d_meridional = to_meridional(d_inverse)
    d_shrunk = jnp.einsum(
        "qmpi,ipx->qmx", meridian, d_meridional, preferred_element_type=jnp.float32
    ).astype(jnp.bfloat16)
    d_blocks, filter_sum_one, filter_sum_two = block_backward(
        blocks, filter_first, filter_second, stored, d_shrunk.reshape(blocks.shape)
    )
    grad_filter_first, grad_filter_second = lax.psum((filter_sum_one, filter_sum_two), "pen")
    d_zonal = jnp.einsum(
        "qmpi,qmx->ipx",
        meridian,
        d_blocks.reshape(2, lat_total, -1),
        preferred_element_type=jnp.float32,
    ).astype(jnp.bfloat16)
    d_zonal_band = to_zonal(d_zonal, band_width)
    d_spatial = jnp.einsum(
        "lqc,jq->ljc", d_zonal_band, forward_zonal, preferred_element_type=jnp.float32
    ).astype(jnp.bfloat16)
    d_spectral = to_column(d_spatial)
    block_output = (
        latents.astype(jnp.float32)
        + spectral_part.astype(jnp.float32)
        + column_mix.reshape(latents.shape)
    ).astype(jnp.bfloat16)
    d_normed = d_column.reshape(latents.shape) + d_spectral.astype(jnp.float32)
    grad_latents = (cotangent.astype(jnp.float32) + pull_norm(d_normed)[0]).astype(jnp.bfloat16)
    return (
        block_output,
        grad_latents,
        grad_weight_in,
        grad_weight_out,
        grad_filter_first,
        grad_filter_second,
    )


def solution(mesh):
    placed = (
        P("pen", "chan", None),
        P(),
        P(("pen", "chan"), None),
        P(("pen", "chan"), None),
        P(None, "chan", None, None),
        P(None, "chan", None, None),
        P("pen", "chan", None),
    )
    return jax.shard_map(
        body,
        mesh=mesh,
        in_specs=placed,
        out_specs=(
            P("pen", "chan", None),
            P("pen", "chan", None),
            P(("pen", "chan"), None),
            P(("pen", "chan"), None),
            P(None, "chan", None, None),
            P(None, "chan", None, None),
        ),
        check_vma=False,
    )
```

profile of v0, /device:TPU:1, one launch (start us, length us, event | category | flops | bytes accessed | tf_op | source)
XLA Modules:
  0.0 2192.8 jit_solution(6108568591293638444)
XLA Ops:
  7.2 4.4 copy.153
  11.6 11.6 all-to-all-start.4
  27.5 32.0 %all-to-all-done.4 = bf16[12,180,256]{1,0,2:T(8,128)(2,1)} async-done(((bf16[12,180,256]{1,0,2:T(8,128)(2,1)}), bf16[12,180,256]{1,0,2:T(8,128)(2,1)}, u32[]{:S(2)}, u32[]{:S(2)}) %all-to-all-start.4) | async-done | bytes 1105952 | tf_op jit(solution)/shard_map/all_to_all | solution.py:130
  59.5 4.4 all-to-all-start
  64.1 10.4 broadcast_multiply_fusion.1
  74.5 3.7 copy.155
  78.2 3.9 all_to_all.98
  82.2 3.7 fusion.70
  86.8 2.8 copy.156
  89.6 4.1 reshape.327
  96.0 45.4 %all-to-all-start.5 = ((bf16[12,2,32,384]{3,1,0,2:T(2,128)(2,1)}), bf16[12,2,32,384]{3,1,0,2:T(2,128)(2,1)}, u32[]{:S(2)}, u32[]{:S(2)}) async-start(bf16[12,2,32,384]{3,1,0,2:T(2,128)(2,1)} %copy.157), calls=%async_computation.5 | async-start | bytes 1179648 | tf_op jit(solution)/shard_map/all_to_all | solution.py:92
  141.4 10.3 sine_negate_fusion
  151.7 3.6 copy.137
  155.3 3.9 all_to_all.87
  159.2 3.7 fusion.68
  163.9 2.8 copy.138
  166.7 4.1 reshape.316
  173.1 7.9 all-to-all-start.1
  181.0 2.3 fusion.65
  183.3 2.6 negate_convert_fusion
  186.1 706.9 %all-gather = bf16[256,4,256]{2,1,0:T(4,128)(2,1)} all-gather(bf16[1,4,256]{2,1,0:T(4,128)(2,1)S(1)} %bitcast.297), channel_id=1, replica_groups=mesh['pen'=32,'chan'=8] {'pen','chan'}, dimensions={0}, use_global_device_ids=true | all-gather | bytes 526336 | tf_op jit(solution)/shard_map/all_gather | solution.py:118
  893.0 2.9 fusion.34
  895.9 4.1 reshape.335
  900.0 3.8 copy.159
  903.9 3.0 fusion.32
  906.9 3.9 reshape.318
  910.8 2.6 convolution_bitcast_fusion.3
  918.0 2.8 copy.162
  920.8 4.1 reshape.331
  924.9 2.9 fusion.37
  927.8 2.9 copy.165
  930.7 7.9 all-to-all-start.6
  938.6 703.1 %all-gather.1 = bf16[256,4,256]{2,1,0:T(4,128)(2,1)} all-gather(bf16[1,4,256]{2,1,0:T(4,128)(2,1)S(1)} %bitcast.298), channel_id=1, replica_groups=mesh['pen'=32,'chan'=8] {'pen','chan'}, dimensions={0}, use_global_device_ids=true | all-gather | bytes 526336 | tf_op jit(solution)/shard_map/all_gather | solution.py:119
  1649.9 7.6 multiply_convert_fusion
  1659.4 4.1 reshape.320
  1667.2 8.0 all-to-all-start.2
  1675.2 9.9 fusion.6
  1686.2 2.4 reshape.333
  1690.6 3.4 fusion.66
  1694.2 6.4 copy.168
  1700.6 9.0 reshape.370
  1709.6 4.4 all-to-all-start.7
  1714.3 4.8 fusion.100
  1719.0 4.7 fusion.99
  1723.8 5.0 fusion.97
  1728.9 2.4 reshape.322
  1733.3 3.4 fusion.72
  1736.9 6.4 copy.148
  1743.3 9.0 reshape.368
  1752.4 8.9 all-to-all-start.3
  1761.3 5.0 fusion.98
  1767.8 2.7 reshape.326
  1770.5 2.7 reshape.324
  1773.3 3.5 copy.151
  1776.7 3.5 copy.170
  1780.2 218.8 %all-reduce.6.cloned.1.call-done = (f32[1024,256]{1,0:T(8,128)}, f32[1024,256]{1,0:T(8,128)}) async-done(((f32[1024,256]{1,0:T(8,128)}, f32[1024,256]{1,0:T(8,128)}), (f32[1024,256]{1,0:T(8,128)}, f32[1024,256]{1,0:T(8,128)})) %all-reduce.6.cloned.1.call-update) | async-done | bytes 2097168
  2003.3 135.2 %all-reduce.3 = (f32[2,1,32,32]{2,3,1,0:T(8,128)S(1)}, f32[2,1,32,32]{2,3,1,0:T(8,128)S(1)}) all-reduce(f32[2,1,32,32]{2,3,1,0:T(8,128)S(1)} %pad_maximum_fusion.1, f32[2,1,32,32]{2,3,1,0:T(8,128)S(1)} %pad_maximum_fusion.2), channel_id=1, replica_groups=mesh['pen'=32,'chan'=8] {'pen'}, use_global_device_ids=true, to_apply=%region_6.7 | all-reduce | flops 4096 | bytes 32768 | tf_op jit(solution)/shard_map/psum | solution.py:179
  2139.9 8.6 reshape.371
  2148.5 7.5 copy.169
  2156.0 8.6 reshape.369
  2164.6 7.5 copy.149
  2172.1 3.8 fusion.18
  2178.3 3.2 add_convert_fusion
  2181.5 2.5 copy.177
  (117 shorter events, 46.1 us)
Async XLA Ops:
  11.6 11.6 copy-start.10
  11.6 48.0 %all-to-all-start.4 = ((bf16[12,180,256]{1,0,2:T(8,128)(2,1)}), bf16[12,180,256]{1,0,2:T(8,128)(2,1)}, u32[]{:S(2)}, u32[]{:S(2)}) async-start(bf16[12,180,256]{1,0,2:T(8,128)(2,1)} %copy.153), calls=%async_computation.4 | async-start | bytes 4194304 | tf_op jit(solution)/shard_map/all_to_all | solution.py:130
  23.8 0.8 copy-start.23
  27.5 36.4 %copy-start.21 = (bf16[2,1,32,32]{3,2,1,0:T(8,128)(2,1)S(1)}, bf16[2,1,32,32]{3,2,1,0:T(8,128)(2,1)}, u32[]{:S(2)}) copy-start(bf16[2,1,32,32]{3,2,1,0:T(8,128)(2,1)} %param.11) | copy-start | bytes 12292
  27.5 36.5 %copy-start.22 = (bf16[2,1,32,32]{3,2,1,0:T(8,128)(2,1)S(1)}, bf16[2,1,32,32]{3,2,1,0:T(8,128)(2,1)}, u32[]{:S(2)}) copy-start(bf16[2,1,32,32]{3,2,1,0:T(8,128)(2,1)} %param.12) | copy-start | bytes 12292
  59.5 36.5 %all-to-all-start = ((bf16[12,180,256]{1,0,2:T(8,128)(2,1)}), bf16[12,180,256]{1,0,2:T(8,128)(2,1)}, u32[]{:S(2)}, u32[]{:S(2)}) async-start(bf16[12,180,256]{1,0,2:T(8,128)(2,1)} %copy.135), calls=%async_computation | async-start | bytes 4194304 | tf_op jit(solution)/shard_map/all_to_all | solution.py:129
  96.0 77.1 %all-to-all-start.5 = ((bf16[12,2,32,384]{3,1,0,2:T(2,128)(2,1)}), bf16[12,2,32,384]{3,1,0,2:T(2,128)(2,1)}, u32[]{:S(2)}, u32[]{:S(2)}) async-start(bf16[12,2,32,384]{3,1,0,2:T(2,128)(2,1)} %copy.157), calls=%async_computation.5 | async-start | bytes 1179648 | tf_op jit(solution)/shard_map/all_to_all | solution.py:92
  173.1 13.0 copy-start.24
  173.1 730.8 %all-to-all-start.1 = ((bf16[12,2,32,384]{3,1,0,2:T(2,128)(2,1)}), bf16[12,2,32,384]{3,1,0,2:T(2,128)(2,1)}, u32[]{:S(2)}, u32[]{:S(2)}) async-start(bf16[12,2,32,384]{3,1,0,2:T(2,128)(2,1)} %copy.139), calls=%async_computation.1 | async-start | bytes 1179648 | tf_op jit(solution)/shard_map/all_to_all | solution.py:92
  186.1 707.0 %copy-start.14 = (bf16[1,384,2,384]{3,1,2,0:T(8,128)(2,1)}, bf16[1,384,2,384]{3,1,2,0:T(8,128)(2,1)S(1)}, u32[]{:S(2)}) copy-start(bf16[1,384,2,384]{3,1,2,0:T(8,128)(2,1)S(1)} %get-tuple-element.40) | copy-start | bytes 1769476
  186.1 707.0 %copy-start.16 = (bf16[1,384,2,384]{3,1,2,0:T(8,128)(2,1)}, bf16[1,384,2,384]{3,1,2,0:T(8,128)(2,1)S(1)}, u32[]{:S(2)}) copy-start(bf16[1,384,2,384]{3,1,2,0:T(8,128)(2,1)S(1)} %get-tuple-element.41) | copy-start | bytes 1769476
  910.8 2.6 copy-start.9
  913.4 1.7 copy-start.7
  915.1 1.0 copy-start.26
  916.0 0.8 copy-start.5
  927.8 10.8 copy-start.25
  930.7 736.4 %all-to-all-start.6 = ((bf16[384,2,1,384]{3,1,2,0:T(2,128)(2,1)}), bf16[384,2,1,384]{3,1,2,0:T(2,128)(2,1)}, u32[]{:S(2)}, u32[]{:S(2)}) async-start(bf16[384,2,1,384]{3,1,2,0:T(2,128)(2,1)} %copy.165), calls=%async_computation.6 | async-start | bytes 1179648 | tf_op jit(solution)/shard_map/all_to_all | solution.py:98
  1645.4 3.4 copy-start.4
  1646.6 10.9 copy-start.18
  1649.9 7.6 copy-start.17
  1657.5 6.0 copy-start.15
  1665.4 9.8 copy-start.11
  1667.2 42.4 %all-to-all-start.2 = ((bf16[384,2,1,384]{3,1,2,0:T(2,128)(2,1)}), bf16[384,2,1,384]{3,1,2,0:T(2,128)(2,1)S(1)}, u32[]{:S(2)}, u32[]{:S(2)}) async-start(bf16[384,2,1,384]{3,1,2,0:T(2,128)(2,1)} %copy.145), calls=%async_computation.2 | async-start | bytes 1179648 | tf_op jit(solution)/shard_map/all_to_all | solution.py:98
  1709.6 4.7 copy-start.12
  1709.6 42.8 %all-to-all-start.7 = ((bf16[8,2,34560]{2,1,0:T(2,128)(2,1)}), bf16[8,2,34560]{2,1,0:T(2,128)(2,1)}, u32[]{:S(2)}, u32[]{:S(2)}) async-start(bf16[8,2,34560]{2,1,0:T(2,128)(2,1)} %reshape.370), calls=%async_computation.7 | async-start | bytes 2211840 | tf_op jit(solution)/shard_map/all_to_all | solution.py:103
  1714.0 285.0 %all-reduce.6.cloned.1.call-start = ((), (), s32[]{:S(2)}) async-start(), calls=%async_computation.8 | async-start | bytes 4194304
  1714.3 4.8 copy-start.13
  1719.0 4.8 copy-start.20
  1743.3 18.0 copy-start.19
  1752.4 403.7 %all-to-all-start.3 = ((bf16[8,2,34560]{2,1,0:T(2,128)(2,1)}), bf16[8,2,34560]{2,1,0:T(2,128)(2,1)}, u32[]{:S(2)}, u32[]{:S(2)}) async-start(bf16[8,2,34560]{2,1,0:T(2,128)(2,1)} %reshape.368), calls=%async_computation.3 | async-start | bytes 2211840 | tf_op jit(solution)/shard_map/all_to_all | solution.py:103
  1761.3 5.0 copy-start.2
  1776.7 223.7 %copy-start.6 = (bf16[2,4608,32,1]{1,2,3,0:T(8,128)(2,1)S(1)}, bf16[2,4608,32,1]{1,2,3,0:T(8,128)(2,1)}, u32[]{:S(2)}) copy-start(bf16[2,4608,32,1]{1,2,3,0:T(8,128)(2,1)} %copy-done.5) | copy-start | bytes 1769476
  1780.2 222.4 %copy-start.8 = (f32[2,4608,1,32]{1,3,0,2:T(8,128)S(1)}, f32[2,4608,1,32]{1,3,0,2:T(8,128)}, u32[]{:S(2)}) copy-start(f32[2,4608,1,32]{1,3,0,2:T(8,128)} %copy-done.7) | copy-start | bytes 3538948
  1999.0 3.6 copy-start.27
  2172.1 4.8 copy-start.1
  2176.0 1.9 copy-start
  2176.0 2.3 copy-start.3
Sparse Core Ops, SparseCore 0:
  1723.9 275.0 all-reduce.5
where the time goes:
time: 2210 us; the launch traced here: 2190 us
  blocking collectives  1550 us (70%)
  waiting for transfers between devices  251 us (11%)
  local copies, waits for them, and re-layouts  175 us (8%)
  starting transfers between devices  98.7 us (4%)
  matrix products  71.1 us (3%)
  other arithmetic  37.1 us (2%)
    all_gather x1, blocking collectives, body(): lax.all_gather(weight_in, ('pen', 'chan'), axis=0, tiled=True)  707 us
    all_gather x1, blocking collectives, body(): lax.all_gather(weight_out, ('pen', 'chan'), axis=0, tiled=True)  703 us
    unnamed x2, waiting for transfers between devices  219 us
    psum x1, blocking collectives, body(): lax.psum((filter_sum_one, filter_sum_two), 'pen')  135 us
    unnamed x72, local copies, waits for them, and re-layouts  54.4 us
    all_to_all x2, starting transfers between devices, to_meridional(): lax.all_to_all(group_modes(modes), 'pen', split_axis=2, concat_axis=0, ti...  53.3 us
  transfers between devices with their start and end apart: 9, of which 2 were waited for; matrix products, arithmetic and copies ran while one was open for 10% of the time, Pallas kernels for 0%

commit v1 on v0

v1 whole, which is shorter than its diff:
```python
import functools
import math

import jax
import jax.numpy as jnp
import ml_dtypes
import numpy as np
from jax import lax
from jax.experimental import pallas as pl
from jax.experimental.pallas import tpu as pltpu
from jax.sharding import PartitionSpec as P

MESH = pl.DeviceIdType.MESH
NLON, KLON, NLAT = 1440, 384, 384
SEG = 180
PAD = 192
RANK = 128
LAT = 12
NK = 12
GELU_C = math.sqrt(2.0 / math.pi)
F32, BF16 = jnp.float32, jnp.bfloat16


def as_bf16(values):
    return np.asarray(values, np.float32).astype(ml_dtypes.bfloat16)


@functools.lru_cache(None)
def tables():
    j = np.arange(NLON)[:, None]
    k = np.arange(KLON)[None, :]
    a = 2.0 * np.pi * ((j * k) % NLON) / NLON
    full = np.concatenate([np.cos(a), -np.sin(a)], axis=1) / math.sqrt(NLON)
    left, _, _ = np.linalg.svd(full[:SEG], full_matrices=False)
    basis = left[:, :RANK]
    expand = np.stack([basis.T @ full[s * SEG : (s + 1) * SEG] for s in range(8)])
    expand = expand.reshape(8, RANK, 2, 32, NK).transpose(3, 2, 4, 0, 1).reshape(768, 8 * RANK)
    basis_pad = np.zeros((PAD, RANK))
    basis_pad[:SEG] = basis
    s = np.arange(32)
    w32 = np.exp(-2j * np.pi * np.outer(s, s) / 32)
    l = np.arange(12)
    w12 = np.exp(-2j * np.pi * np.outer(l, l) / 12)

    def real_form(w):
        return np.stack(
            [np.stack([w.real, -w.imag], axis=1), np.stack([w.imag, w.real], axis=1)]
        )

    first = np.einsum("qmps,kl->qmkspl", real_form(w32), np.eye(NK)).reshape(768, 768)
    second = np.einsum("qmpl,cd->plcqmd", real_form(w12), np.eye(32)).reshape(768, 768)
    twiddle = np.exp(-2j * np.pi * np.outer(s, l) / 384) / math.sqrt(NLAT)
    twiddle = np.repeat(np.repeat(twiddle, NK, axis=0), 32, axis=1)
    return dict(
        basis=as_bf16(basis_pad),
        expand=as_bf16(expand),
        first=as_bf16(first),
        first_t=as_bf16(first.T),
        second=as_bf16(second),
        second_t=as_bf16(second.T),
        tw_re=np.asarray(twiddle.real, np.float32),
        tw_im=np.asarray(twiddle.imag, np.float32),
    )


CONSTS = ("basis", "expand", "first", "first_t", "second", "second_t", "tw_re", "tw_im")


def dot(a, b, ca=1, cb=0):
    return lax.dot_general(a, b, (((ca,), (cb,)), ((), ())), preferred_element_type=F32)


def gelu_parts(v):
    v2 = v * v
    t = jnp.tanh(v * (GELU_C + (GELU_C * 0.044715) * v2))
    half = 0.5 + 0.5 * t
    value = v * half
    slope = half + (0.5 * v) * (1.0 - t * t) * (GELU_C + (3.0 * GELU_C * 0.044715) * v2)
    return value, slope


class Push:
    def __init__(self, send_sem, recv_sem):
        self.send_sem, self.recv_sem, self.copies = send_sem, recv_sem, []

    def start(self, src, dst, device):
        n = len(self.copies)
        copy = pltpu.make_async_remote_copy(
            src_ref=src,
            dst_ref=dst,
            send_sem=self.send_sem.at[n],
            recv_sem=self.recv_sem.at[n],
            device_id=device,
            device_id_type=MESH,
        )
        copy.start()
        self.copies.append(copy)

    def wait_recv(self):
        for copy in self.copies:
            copy.wait_recv()

    def wait_send(self):
        for copy in self.copies:
            copy.wait_send()


def kernel(*refs):
    (lat_ref, gain_ref, win_ref, wout_ref, ff_ref, fs_ref, cot_ref) = refs[:7]
    const_hbm = refs[7 : 7 + len(CONSTS)]
    refs = refs[7 + len(CONSTS) :]
    (bo_ref, gl_ref, gwi_ref, gwo_ref, gff_ref, gfs_ref) = refs[:6]
    refs = refs[6:]
    const = refs[: len(CONSTS)]
    refs = refs[len(CONSTS) :]
    (normed_s, cot_s, send1, recv1, send2, recv2, send3, recv3, send4, recv4) = refs[:10]
    (cm_s, dc_s, zsrc, zbuf, pk, wfull, gacc, gsc, grc, gsx, grx, gsz, grz) = refs[10:23]
    (fbuf, frc, fry, frz) = refs[23:27]
    (const_sem, s1s, s1r, s2s, s2r, s3s, s3r, s4s, s4r) = refs[27:36]
    (wzs, wzr, wxs, wxr, wcs, wcr, gzs, gzr, gxs, gxr, gcs, gcr) = refs[36:48]
    (fcs, fcr, fys, fyr, fzs, fzr) = refs[48:54]
    V, expand, first, first_t, second, second_t, tw_re, tw_im = const

    pen = lax.axis_index("pen")
    chan = lax.axis_index("chan")
    x, zhi = chan // 2, lax.rem(chan, 2)
    y, zlo, core = pen // 8, lax.rem(pen // 2, 4), lax.rem(pen, 2)
    z = zhi * 4 + zlo
    xy = x * 4 + y

    def device(x_, y_, z_, core_):
        return (y_ * 8 + lax.rem(z_, 4) * 2 + core_, x_ * 2 + z_ // 4)

    chan_peers = [(pen, lax.rem(chan + d, 8)) for d in range(1, 8)]
    pen_peers = [(lax.rem(pen + d, 32), chan) for d in range(1, 32)]
    z_index = [lax.rem(z + d, 8) for d in range(1, 8)]
    z_peers = [device(x, y, i, core) for i in z_index]
    xy_index = [lax.rem(xy + d, 16) for d in range(1, 16)]
    xy_peers = [device(i // 4, lax.rem(i, 4), z, core) for i in xy_index]
    sibling = device(x, y, z, 1 - core)
    y_peers = [device(x, lax.rem(y + d, 4), z, core) for d in range(1, 4)]
    zlo_peers = [device(x, y, zhi * 4 + lax.rem(zlo + d, 4), core) for d in range(1, 4)]

    loads = []
    for n, (src, dst) in enumerate(zip(const_hbm, const)):
        load = pltpu.make_async_copy(src, dst, const_sem.at[n])
        load.start()
        loads.append(load)
    loads = dict(zip(CONSTS, loads))

    barrier = pltpu.get_barrier_semaphore()
    greeted = chan_peers + pen_peers + z_peers + xy_peers
    for peer in greeted:
        pl.semaphore_signal(barrier, inc=1, device_id=peer, device_id_type=MESH)

    zsrc[0:4, :] = win_ref[...].astype(F32)
    zsrc[4:8, :] = wout_ref[...].astype(F32)
    zbuf[z] = zsrc[...]
    normed_s[:, 176:192, :] = jnp.zeros((LAT, 16, 256), BF16)
    cot_s[:, 176:192, :] = jnp.zeros((LAT, 16, 256), BF16)
    pl.semaphore_wait(barrier, len(greeted))

    w_z = Push(wzs, wzr)
    for peer in z_peers:
        w_z.start(zsrc, zbuf.at[z], peer)

    loads["basis"].wait()

    def compress(rows, slot, l):
        coded = dot(rows, V[...], 0, 0).astype(BF16)
        send1[slot, :, l] = coded.reshape(8, 32, RANK)

    def cot_row(l, carry):
        cot_s[l, 0:SEG] = cot_ref[l]
        compress(cot_s[l], 1, l)
        return carry

    lax.fori_loop(0, LAT, cot_row, 0)
    ex1 = [None, None]
    ex1[1] = Push(s1s.at[1], s1r.at[1])
    for d, peer in enumerate(chan_peers):
        ex1[1].start(send1.at[1, peer[1]], recv1.at[1, chan], peer)
    recv1[1, chan] = send1[1, chan]

    w_z.wait_recv()
    pk[0] = jnp.concatenate([zbuf[i, 0:4] for i in range(8)], axis=0).astype(BF16)
    pk[1] = jnp.concatenate([zbuf[i, 4:8] for i in range(8)], axis=0).astype(BF16)
    wfull[core, xy] = pk[...]
    w_x = Push(wxs, wxr)
    for peer in xy_peers:
        w_x.start(pk, wfull.at[core, xy], peer)

    def norm_row(l, carry):
        values = lat_ref[l].astype(F32)
        centred = values - jnp.mean(values, axis=-1, keepdims=True)
        spread = jnp.mean(centred * centred, axis=-1, keepdims=True)
        normed_s[l, 0:SEG] = (centred * lax.rsqrt(spread + 1e-05) * gain_ref[...]).astype(BF16)
        compress(normed_s[l], 0, l)
        return carry

    lax.fori_loop(0, LAT, norm_row, 0)
    ex1[0] = Push(s1s.at[0], s1r.at[0])
    for d, peer in enumerate(chan_peers):
        ex1[0].start(send1.at[0, peer[1]], recv1.at[0, chan], peer)
    recv1[0, chan] = send1[0, chan]

    w_x.wait_recv()
    w_c = Push(wcs, wcr)
    w_c.start(wfull.at[core], wfull.at[core], sibling)
    cm_s[...] = jnp.zeros_like(cm_s)
    dc_s[...] = jnp.zeros_like(dc_s)
    gacc[...] = jnp.zeros_like(gacc)
    w_c.wait_recv()

    def mlp_step(i, carry):
        t, h = i // 4, lax.rem(i, 4)
        half, part = h // 2, pl.ds(lax.rem(h, 2) * 8, 8)
        rows = pl.ds(t * 4, 4)
        tokens = normed_s[rows].reshape(4 * PAD, 256)
        grads = cot_s[rows].reshape(4 * PAD, 256)
        w_in = wfull[half, part, 0].reshape(256, 256)
        w_out = wfull[half, part, 1].reshape(256, 256)
        value, slope = gelu_parts(dot(tokens, w_in, 1, 1))
        hidden = value.astype(BF16)
        d_pre = (dot(grads, w_out, 1, 1) * slope).astype(BF16)
        cm_s[rows] += dot(hidden, w_out).reshape(4, PAD, 256)
        dc_s[rows] += dot(d_pre, w_in).reshape(4, PAD, 256)
        gacc[half, part, 0] += dot(d_pre, tokens, 0, 0).reshape(8, 32, 256)
        gacc[half, part, 1] += dot(hidden, grads, 0, 0).reshape(8, 32, 256)
        return carry

    lax.fori_loop(0, 12, mlp_step, 0)
    gsc[...] = gacc[1 - core].astype(BF16)
    g_c = Push(gcs, gcr)
    g_c.start(gsc, grc, sibling)

    loads["expand"].wait()
    row = lax.broadcasted_iota(jnp.int32, (768, 1), 0)
    weight = jnp.where((row == 0) | (row == 12), 1.0, 2.0).astype(F32)

    def zonal(slot):
        ex1[slot].wait_recv()
        coded = jnp.concatenate([recv1[slot, i].reshape(384, RANK) for i in range(8)], axis=1)
        return dot(expand[...], coded, 1, 1)

    modes_1 = (zonal(1) * weight).reshape(32, 24, 384)
    modes_0 = zonal(0).reshape(32, 24, 384)
    send2[...] = jnp.concatenate([modes_0, modes_1], axis=1).astype(BF16)
    ex2 = Push(s2s, s2r)
    for peer in pen_peers:
        ex2.start(send2.at[peer[0]], recv2.at[pen], peer)
    recv2[pen] = send2[pen]

    g_c.wait_recv()
    gsx[...] = (gacc[core] + grc[...].astype(F32)).astype(BF16)
    g_x = Push(gxs, gxr)
    for index, peer in zip(xy_index, xy_peers):
        g_x.start(gsx.at[index], grx.at[xy], peer)
    grx[xy] = gsx[xy]

    r128 = lax.broadcasted_iota(jnp.int32, (128, 128), 0) // 32
    c128 = lax.broadcasted_iota(jnp.int32, (128, 128), 1) // 32
    block = (r128 == c128).astype(F32)

    def spread_filter(ref):
        parts = []
        for part in range(2):
            w = ref[part].astype(F32)
            w = jnp.concatenate([w] * 4, axis=1)
            parts.append(jnp.concatenate([w] * 4, axis=0) * block)
        re, im = parts
        top = jnp.concatenate([re, im], axis=1)
        low = jnp.concatenate([-im, re], axis=1)
        return jnp.concatenate([top, low], axis=0).astype(BF16)

    filter_1 = spread_filter(ff_ref)
    filter_2 = spread_filter(fs_ref)
    for name in ("first", "first_t", "second", "second_t", "tw_re", "tw_im"):
        loads[name].wait()

    def meridian(modes):
        out = dot(first[...], modes)
        re, im = out[:384], out[384:]
        g_re = re * tw_re[...] - im * tw_im[...]
        g_im = re * tw_im[...] + im * tw_re[...]
        mixed = jnp.concatenate([g_re, g_im], axis=1).astype(BF16)
        out = dot(mixed, second[...])
        return jnp.concatenate(
            [
                jnp.concatenate(
                    [out[:, g * 128 : g * 128 + 128], out[:, 384 + g * 128 : 512 + g * 128]], axis=1
                )
                for g in range(3)
            ],
            axis=0,
        )

    def meridian_back(spectra):
        spectra = jnp.concatenate(
            [spectra[g * 384 : g * 384 + 384, :128] for g in range(3)]
            + [spectra[g * 384 : g * 384 + 384, 128:] for g in range(3)],
            axis=1,
        )
        out = dot(spectra, second_t[...])
        re, im = out[:, :384], out[:, 384:]
        h_re = re * tw_re[...] + im * tw_im[...]
        h_im = im * tw_re[...] - re * tw_im[...]
        mixed = jnp.concatenate([h_re, h_im], axis=0).astype(BF16)
        return dot(first_t[...], mixed)

    ex2.wait_recv()
    received = recv2[...].astype(F32)
    spectrum = meridian(received[:, :24].reshape(768, 384).astype(BF16)).astype(BF16)
    d_shrunk = meridian(received[:, 24:].reshape(768, 384).astype(BF16))
    value, slope = gelu_parts(dot(spectrum, filter_1))
    first_hidden = value.astype(BF16)
    second_act = dot(first_hidden, filter_2)
    bend = jnp.tanh(second_act * 10.0)
    shrunk = (second_act - 0.1 * bend).astype(BF16)
    d_second = (d_shrunk * bend * bend).astype(BF16)
    outer_2 = dot(first_hidden, d_second, 0, 0)
    d_first = (dot(d_second, filter_2, 1, 1) * slope).astype(BF16)
    outer_1 = dot(spectrum, d_first, 0, 0)
    d_spectrum = dot(d_first, filter_1, 1, 1).astype(BF16)
    back_0 = meridian_back(shrunk).reshape(32, 24, 384)
    back_1 = meridian_back(d_spectrum).reshape(32, 24, 384)
    send3[...] = jnp.concatenate([back_0, back_1], axis=1).astype(BF16)
    ex3 = Push(s3s, s3r)
    for peer in pen_peers:
        ex3.start(send3.at[peer[0]], recv3.at[pen], peer)
    recv3[pen] = send3[pen]

    lane_group = lax.broadcasted_iota(jnp.int32, (32, 128), 1) // 32

    def fold(outer):
        o = {}
        for p in range(2):
            for q in range(2):
                tile = outer[p * 128 : p * 128 + 128, q * 128 : q * 128 + 128] * block
                tile = tile[0:32] + tile[32:64] + tile[64:96] + tile[96:128]
                tile = tile + pltpu.roll(tile, 64, 1)
                o[p, q] = tile + pltpu.roll(tile, 32, 1)
        return o[0, 0] + o[1, 1], o[0, 1] - o[1, 0]

    f1_re, f1_im = fold(outer_1)
    f2_re, f2_im = fold(outer_2)
    mine = jnp.where(
        lane_group == 0, f1_re, jnp.where(lane_group == 1, f1_im, jnp.where(lane_group == 2, f2_re, f2_im))
    )
    fbuf[0] = mine
    f_c = Push(fcs, fcr)
    f_c.start(fbuf.at[0], frc, sibling)

    g_x.wait_recv()
    summed = grx[0].astype(F32)
    for i in range(1, 16):
        summed = summed + grx[i].astype(F32)
    for i in range(8):
        gsz[i, 0:4] = summed[0, i * 4 : i * 4 + 4]
        gsz[i, 4:8] = summed[1, i * 4 : i * 4 + 4]
    g_z = Push(gzs, gzr)
    for index, peer in zip(z_index, z_peers):
        g_z.start(gsz.at[index], grz.at[z], peer)
    grz[z] = gsz[z]

    f_c.wait_recv()
    fbuf[1] = fbuf[0] + frc[...]
    f_y = Push(fys, fyr)
    for peer in y_peers:
        f_y.start(fbuf.at[1], fry.at[y], peer)
    fry[y] = fbuf[1]
    f_y.wait_recv()
    fbuf[2] = (fry[0] + fry[1]) + (fry[2] + fry[3])
    f_z = Push(fzs, fzr)
    for peer in zlo_peers:
        f_z.start(fbuf.at[2], frz.at[zlo], peer)
    frz[zlo] = fbuf[2]
    g_z.wait_recv()
    total = grz[0]
    for i in range(1, 8):
        total = total + grz[i]
    gwi_ref[...] = total[0:4]
    gwo_ref[...] = total[4:8]
    f_z.wait_recv()
    total = (frz[0] + frz[1]) + (frz[2] + frz[3])
    gff_ref[0] = total[:, 0:32]
    gff_ref[1] = total[:, 32:64]
    gfs_ref[0] = total[:, 64:96]
    gfs_ref[1] = total[:, 96:128]

    ex3.wait_recv()
    received = recv3[...].astype(F32)

    def unzonal(modes, slot):
        coded = dot(modes, expand[...], 0, 0).astype(BF16)
        for i in range(8):
            send4[slot, i] = coded[:, i * RANK : i * RANK + RANK].reshape(LAT, 32, RANK)
        push = Push(s4s.at[slot], s4r.at[slot])
        for peer in chan_peers:
            push.start(send4.at[slot, peer[1]], recv4.at[slot, chan], peer)
        recv4[slot, chan] = send4[slot, chan]
        return push

    ex4 = [None, None]
    ex4[0] = unzonal((received[:, :24].reshape(768, 384) * weight).astype(BF16), 0)
    ex4[1] = unzonal(received[:, 24:].reshape(768, 384).astype(BF16), 1)

    ex4[0].wait_recv()

    def out_row(l, carry):
        coded = recv4[0, :, l].reshape(256, RANK)
        spatial = dot(V[...], coded, 1, 1)[:SEG]
        bo_ref[l] = (lat_ref[l].astype(F32) + spatial + cm_s[l, 0:SEG]).astype(BF16)
        return carry

    lax.fori_loop(0, LAT, out_row, 0)
    ex4[1].wait_recv()

    def grad_row(l, carry):
        coded = recv4[1, :, l].reshape(256, RANK)
        d_normed = dot(V[...], coded, 1, 1)[:SEG] + dc_s[l, 0:SEG]
        values = lat_ref[l].astype(F32)
        centred = values - jnp.mean(values, axis=-1, keepdims=True)
        spread = jnp.mean(centred * centred, axis=-1, keepdims=True)
        scale = lax.rsqrt(spread + 1e-05)
        unit = centred * scale
        d_unit = d_normed * gain_ref[...]
        mean_d = jnp.mean(d_unit, axis=-1, keepdims=True)
        mean_du = jnp.mean(d_unit * unit, axis=-1, keepdims=True)
        d_values = scale * (d_unit - mean_d - unit * mean_du)
        gl_ref[l] = (cot_ref[l].astype(F32) + d_values).astype(BF16)
        return carry

    lax.fori_loop(0, LAT, grad_row, 0)
    for push in (w_z, w_x, w_c, g_c, g_x, g_z, f_c, f_y, f_z, ex1[0], ex1[1], ex2, ex3, ex4[0], ex4[1]):
        push.wait_send()


def body(latents, norm_gain, weight_in, weight_out, filter_first, filter_second, cotangent):
    table = tables()
    consts = [jnp.asarray(table[name]) for name in CONSTS]
    dma = pltpu.SemaphoreType.DMA
    vmem = pl.BlockSpec(memory_space=pltpu.VMEM)
    scratch = [pltpu.VMEM(c.shape, c.dtype) for c in consts]
    scratch += [
        pltpu.VMEM((LAT, PAD, 256), BF16),
        pltpu.VMEM((LAT, PAD, 256), BF16),
        pltpu.VMEM((2, 8, LAT, 32, RANK), BF16),
        pltpu.VMEM((2, 8, LAT, 32, RANK), BF16),
        pltpu.VMEM((32, 48, 384), BF16),
        pltpu.VMEM((32, 48, 384), BF16),
        pltpu.VMEM((32, 48, 384), BF16),
        pltpu.VMEM((32, 48, 384), BF16),
        pltpu.VMEM((2, 8, LAT, 32, RANK), BF16),
        pltpu.VMEM((2, 8, LAT, 32, RANK), BF16),
        pltpu.VMEM((LAT, PAD, 256), F32),
        pltpu.VMEM((LAT, PAD, 256), F32),
        pltpu.VMEM((8, 256), F32),
        pltpu.VMEM((8, 8, 256), F32),
        pltpu.VMEM((2, 32, 256), BF16),
        pltpu.VMEM((2, 16, 2, 32, 256), BF16),
        pltpu.VMEM((2, 16, 2, 32, 256), F32),
        pltpu.VMEM((16, 2, 32, 256), BF16),
        pltpu.VMEM((16, 2, 32, 256), BF16),
        pltpu.VMEM((16, 2, 32, 256), BF16),
        pltpu.VMEM((16, 2, 32, 256), BF16),
        pltpu.VMEM((8, 8, 256), F32),
        pltpu.VMEM((8, 8, 256), F32),
        pltpu.VMEM((3, 32, 128), F32),
        pltpu.VMEM((32, 128), F32),
        pltpu.VMEM((4, 32, 128), F32),
        pltpu.VMEM((4, 32, 128), F32),
    ]
    scratch += [dma((len(CONSTS),))]
    scratch += [dma((2, 7)), dma((2, 7)), dma((31,)), dma((31,)), dma((31,)), dma((31,)), dma((2, 7)), dma((2, 7))]
    for n in (7, 15, 1, 7, 15, 1, 1, 3, 3):
        scratch += [dma((n,)), dma((n,))]
    out_shape = (
        jax.ShapeDtypeStruct(latents.shape, BF16),
        jax.ShapeDtypeStruct(latents.shape, BF16),
        jax.ShapeDtypeStruct((4, 256), F32),
        jax.ShapeDtypeStruct((4, 256), F32),
        jax.ShapeDtypeStruct((2, 32, 32), F32),
        jax.ShapeDtypeStruct((2, 32, 32), F32),
    )
    outs = pl.pallas_call(
        kernel,
        out_shape=out_shape,
        in_specs=[vmem] * 7 + [pl.BlockSpec(memory_space=pl.ANY)] * len(CONSTS),
        out_specs=(vmem,) * 6,
        scratch_shapes=scratch,
        compiler_params=pltpu.CompilerParams(
            collective_id=0, has_side_effects=True, vmem_limit_bytes=62 * 1024 * 1024
        ),
        name="spectral_block",
    )(
        latents,
        norm_gain.reshape(1, 256),
        weight_in,
        weight_out,
        filter_first.reshape(2, 32, 32),
        filter_second.reshape(2, 32, 32),
        cotangent,
        *consts,
    )
    return outs[:4] + (outs[4].reshape(2, 1, 32, 32), outs[5].reshape(2, 1, 32, 32))


def solution(mesh):
    placed = (
        P("pen", "chan", None),
        P(),
        P(("pen", "chan"), None),
        P(("pen", "chan"), None),
        P(None, "chan", None, None),
        P(None, "chan", None, None),
        P("pen", "chan", None),
    )
    return jax.shard_map(
        body,
        mesh=mesh,
        in_specs=placed,
        out_specs=(
            P("pen", "chan", None),
            P("pen", "chan", None),
            P(("pen", "chan"), None),
            P(("pen", "chan"), None),
            P(None, "chan", None, None),
            P(None, "chan", None, None),
        ),
        check_vma=False,
    )
```

time: 2210 us -> 169 us (0.08)
  blocking collectives: 1550 us -> 0 us
  waiting for transfers between devices: 251 us -> 0 us
  local copies, waits for them, and re-layouts: 175 us -> 5.85 us
  Pallas kernels: 0 us -> 162 us
  starting transfers between devices: 98.7 us -> 0 us
  matrix products: 71.1 us -> 0 us
  other arithmetic: 37.1 us -> 0 us
    all_gather x2 -> x0, blocking collectives: 1410 us -> none  [the longest x1 707 us: body(): lax.all_gather(weight_in, ('pen', 'chan'), axis=0, tiled=True)]
    unnamed x2 -> x0, waiting for transfers between devices: 219 us -> none
    pallas_call x0 -> x1, Pallas kernels: none -> 162 us  [body(): pl.pallas_call(kernel, out_shape=out_shape, in_specs=[vmem] * 7 + [pl.Blo...]
    psum x1 -> x0, blocking collectives: 135 us -> none  [body(): lax.psum((filter_sum_one, filter_sum_two), 'pen')]
    all_to_all x8 -> x0, starting transfers between devices: 98.4 us -> none  [the longest x2 53.3 us: to_meridional(): lax.all_to_all(group_modes(modes), 'pen', split_axis=2, concat_axis=0, ti...]
    dot_general x16 -> x0, matrix products: 56.8 us -> none  [the longest x1 9.86 us: body(): lax.dot_general(grad_tokens, full_out, (((1,), (1,)), ((), ())), preferre...]
    reshape x18 -> x0, local copies, waits for them, and re-layouts: 50.1 us -> none  [the longest x4 12.8 us: group_modes(): return modes.reshape(modes.shape[0], 2, lax.axis_size('pen'), -1)]
    convert_element_type x12 -> x0, local copies, waits for them, and re-layouts: 49.8 us -> none  [the longest x2 7.92 us: block_backward(): d_shrunk.astype(jnp.float32) * slope * slope]
  transfers between devices with their start and end apart: 9 -> 0, of which waited for: 2 -> 0; matrix products, arithmetic and copies ran while one was open for 10% -> 0% of each run, Pallas kernels for 0% -> 0%
where the time goes in v1:
time: 169 us
  Pallas kernels  162 us (96%)
  local copies, waits for them, and re-layouts  5.85 us (3%)
    pallas_call x1, Pallas kernels, body(): pl.pallas_call(kernel, out_shape=out_shape, in_specs=[vmem] * 7 + [pl.Blo...  162 us
    unnamed x16, local copies, waits for them, and re-layouts  5.85 us

profile of v1, /device:TPU:1, one launch (start us, length us, event | category | flops | bytes accessed | tf_op | source)
XLA Modules:
  0.0 168.8 jit_solution(10008229864090114461)
XLA Ops:
  0.6 162.3 %spectral_block.1 = (bf16[12,180,256]{2,1,0:T(8,128)(2,1)}, bf16[12,180,256]{2,1,0:T(8,128)(2,1)}, f32[4,256]{1,0:T(4,128)}, f32[4,256]{1,0:T(4,128)}, f32[2,32,32]{2,1,0:T(8,128)}, /*index=5*/f32[2,32,32]{2,1,0:T(8,128)}) custom-call(bf16[12,180,256]{2,1,0:T(8,128)(2,1)} %refs_0_.1, f32[1,256]{1,0:T(1,128)} %bitcast.13, bf16[4,256]{1,0:T(4,128)(2,1)} %refs_2_.1, ...), custom_call_target="tpu_custom_call" | custom-call | tf_op jit(solution)/shard_map/spectral_block/pallas_call | solution.py:486
  162.9 0.0 copy-start
  162.9 2.4 %copy.29 = bf16[12,180,256]{2,1,0:T(8,128)(2,1)} copy(bf16[12,180,256]{2,1,0:T(8,128)(2,1)} %get-tuple-element.30) | data formatting | bytes 2211840
  165.3 0.0 copy-done
  165.3 0.0 copy-start.4
  165.3 0.0 copy-start.3
  165.3 0.0 copy-start.2
  165.4 0.0 copy-start.1
  165.4 1.0 copy.30
  166.4 0.0 copy-done.4
  166.4 0.6 copy.31
  167.0 0.0 copy-done.3
  167.0 0.6 copy.32
  167.6 0.0 copy-done.2
  167.6 0.6 copy.33
  168.2 0.0 copy-done.1
  168.2 0.6 copy.34
Async XLA Ops:
  162.9 2.4 %copy-start = (bf16[12,180,256]{2,1,0:T(8,128)(2,1)S(1)}, bf16[12,180,256]{2,1,0:T(8,128)(2,1)}, u32[]{:S(2)}) copy-start(bf16[12,180,256]{2,1,0:T(8,128)(2,1)} %get-tuple-element.31) | copy-start | bytes 3317764
  165.3 1.0 copy-start.4
  165.3 1.6 copy-start.3
  165.3 2.2 %copy-start.2 = (f32[2,32,32]{2,1,0:T(8,128)S(1)}, f32[2,32,32]{2,1,0:T(8,128)}, u32[]{:S(2)}) copy-start(f32[2,32,32]{2,1,0:T(8,128)} %get-tuple-element.16) | copy-start | bytes 24580
  165.4 2.8 %copy-start.1 = (f32[2,32,32]{2,1,0:T(8,128)S(1)}, f32[2,32,32]{2,1,0:T(8,128)}, u32[]{:S(2)}) copy-start(f32[2,32,32]{2,1,0:T(8,128)} %get-tuple-element.17) | copy-start | bytes 24580

commit v2 on v1

v2 whole, which is shorter than its diff:
```python
import functools
import math

import jax
import jax.numpy as jnp
import ml_dtypes
import numpy as np
from jax import lax
from jax.experimental import pallas as pl
from jax.experimental.pallas import tpu as pltpu
from jax.sharding import PartitionSpec as P

MESH = pl.DeviceIdType.MESH
NLON, KLON, NLAT = 1440, 384, 384
SEG = 180
PAD = 192
RANK = 128
LAT = 12
NK = 12
GELU_C = math.sqrt(2.0 / math.pi)
F32, BF16 = jnp.float32, jnp.bfloat16


def as_bf16(values):
    return np.asarray(values, np.float32).astype(ml_dtypes.bfloat16)


@functools.lru_cache(None)
def tables():
    j = np.arange(NLON)[:, None]
    k = np.arange(KLON)[None, :]
    a = 2.0 * np.pi * ((j * k) % NLON) / NLON
    full = np.concatenate([np.cos(a), -np.sin(a)], axis=1) / math.sqrt(NLON)
    left, _, _ = np.linalg.svd(full[:SEG], full_matrices=False)
    basis = left[:, :RANK]
    expand = np.stack([basis.T @ full[s * SEG : (s + 1) * SEG] for s in range(8)])
    expand = expand.reshape(8, RANK, 2, 32, NK).transpose(3, 2, 4, 0, 1).reshape(768, 8 * RANK)
    basis_pad = np.zeros((PAD, RANK))
    basis_pad[:SEG] = basis
    s = np.arange(32)
    w32 = np.exp(-2j * np.pi * np.outer(s, s) / 32)
    l = np.arange(12)
    w12 = np.exp(-2j * np.pi * np.outer(l, l) / 12)

    def real_form(w):
        return np.stack(
            [np.stack([w.real, -w.imag], axis=1), np.stack([w.imag, w.real], axis=1)]
        )

    first = np.einsum("qmps,kl->qmkspl", real_form(w32), np.eye(NK)).reshape(768, 768)
    second = np.einsum("qmpl,cd->plcqmd", real_form(w12), np.eye(32)).reshape(768, 768)
    twiddle = np.exp(-2j * np.pi * np.outer(s, l) / 384) / math.sqrt(NLAT)
    twiddle = np.repeat(np.repeat(twiddle, NK, axis=0), 32, axis=1)
    return dict(
        basis=as_bf16(basis_pad),
        expand=as_bf16(expand),
        first=as_bf16(first),
        first_t=as_bf16(first.T),
        second=as_bf16(second),
        second_t=as_bf16(second.T),
        tw_re=np.asarray(twiddle.real, np.float32),
        tw_im=np.asarray(twiddle.imag, np.float32),
    )


CONSTS = ("basis", "expand", "first", "first_t", "second", "second_t", "tw_re", "tw_im")


def dot(a, b, ca=1, cb=0):
    return lax.dot_general(a, b, (((ca,), (cb,)), ((), ())), preferred_element_type=F32)


def gelu_parts(v):
    v2 = v * v
    t = jnp.tanh(v * (GELU_C + (GELU_C * 0.044715) * v2))
    half = 0.5 + 0.5 * t
    value = v * half
    slope = half + (0.5 * v) * (1.0 - t * t) * (GELU_C + (3.0 * GELU_C * 0.044715) * v2)
    return value, slope


class Push:
    def __init__(self, send_sem, recv_sem):
        self.send_sem, self.recv_sem, self.copies = send_sem, recv_sem, []

    def start(self, src, dst, device):
        n = len(self.copies)
        copy = remote(src, dst, self.send_sem.at[n], self.recv_sem.at[n], device)
        copy.start()
        self.copies.append(copy)

    def wait_recv(self):
        for copy in self.copies:
            copy.wait_recv()

    def wait_send(self):
        for copy in self.copies:
            copy.wait_send()


def remote(src, dst, send_sem, recv_sem, device):
    return pltpu.make_async_remote_copy(
        src_ref=src,
        dst_ref=dst,
        send_sem=send_sem,
        recv_sem=recv_sem,
        device_id=device,
        device_id_type=MESH,
    )


def kernel(*refs):
    (lat_ref, gain_ref, win_ref, wout_ref, ff_ref, fs_ref, cot_ref) = refs[:7]
    const_hbm = refs[7 : 7 + len(CONSTS)]
    refs = refs[7 + len(CONSTS) :]
    (bo_ref, gl_ref, gwi_ref, gwo_ref, gff_ref, gfs_ref) = refs[:6]
    refs = refs[6:]
    const = refs[: len(CONSTS)]
    refs = refs[len(CONSTS) :]
    (normed_s, cot_s, send1, recv1, send2, recv2, send3, recv3, send4, mid4, recv4) = refs[:11]
    (mixed_s, cm_s, dc_s, zsrc, zbuf, pk, wfull, gacc, gsc, grc, gsx, grx, gsz, grz) = refs[11:25]
    (fsrc, fpair, fall, fbuf, frc, frx, frz) = refs[25:32]
    (const_sem, s1s, s1r, s2s, s2r, s3s, s3r, s4s, s4r, s5s, s5r) = refs[32:43]
    (wzs, wzr, wxs, wxr, wcs, wcr, gzs, gzr, gxs, gxr, gcs, gcr) = refs[43:55]
    (fps, fpr, fas, far, fcs, fcr, fxs, fxr, fzs, fzr) = refs[55:65]
    V, expand, first, first_t, second, second_t, tw_re, tw_im = const

    pen = lax.axis_index("pen")
    chan = lax.axis_index("chan")
    x, zhi = chan // 2, lax.rem(chan, 2)
    y, zlo, core = pen // 8, lax.rem(pen // 2, 4), lax.rem(pen, 2)
    z = zhi * 4 + zlo
    xy = x * 4 + y
    place = y * 8 + x * 2 + core

    def device(x_, y_, z_, core_):
        return (y_ * 8 + lax.rem(z_, 4) * 2 + core_, x_ * 2 + z_ // 4)

    def member(p):
        return device(lax.rem(p // 2, 4), p // 8, z, lax.rem(p, 2))

    def same(device_):
        return (device_[0] == pen) & (device_[1] == chan)

    z_index = [lax.rem(z + d, 8) for d in range(1, 8)]
    z_peers = [device(x, y, i, core) for i in z_index]
    xy_index = [lax.rem(xy + d, 16) for d in range(1, 16)]
    xy_peers = [device(i // 4, lax.rem(i, 4), z, core) for i in xy_index]
    place_index = [lax.rem(place + d, 32) for d in range(1, 32)]
    place_peers = [member(p) for p in place_index]
    sibling = device(x, y, z, 1 - core)
    x_index = [lax.rem(x + d, 4) for d in range(1, 4)]
    x_peers = [device(i, y, z, core) for i in x_index]
    z_partner = device(x, y, (1 - zhi) * 4 + zlo, core)
    to_index = [lax.rem(z + d, 8) for d in (4, 1, 7, 2, 6, 3, 5, 0)]
    to_devices = [device(zlo, y, i, core) for i in to_index]
    from_devices = [device(i // 2, y, (i % 2) * 4 + x, core) for i in range(8)]

    loads = []
    for n, (src, dst) in enumerate(zip(const_hbm, const)):
        load = pltpu.make_async_copy(src, dst, const_sem.at[n])
        load.start()
        loads.append(load)
    loads = dict(zip(CONSTS, loads))

    barrier = pltpu.get_barrier_semaphore()
    for peer in place_peers + z_peers:
        pl.semaphore_signal(barrier, inc=1, device_id=peer, device_id_type=MESH)
    for peer in from_devices:

        @pl.when(jnp.logical_not(same(peer)))
        def _():
            pl.semaphore_signal(barrier, inc=1, device_id=peer, device_id_type=MESH)

    zsrc[0:4, :] = win_ref[...].astype(F32)
    zsrc[4:8, :] = wout_ref[...].astype(F32)
    zbuf[z] = zsrc[...]
    fsrc[...] = jnp.concatenate(
        [ff_ref[0].astype(F32), ff_ref[1].astype(F32), fs_ref[0].astype(F32), fs_ref[1].astype(F32)],
        axis=1,
    )
    fpair[zhi] = fsrc[...]
    normed_s[:, 176:192, :] = jnp.zeros((LAT, 16, 256), BF16)
    cot_s[:, 176:192, :] = jnp.zeros((LAT, 16, 256), BF16)
    own = jnp.where(x == zlo, 1, 0)
    pl.semaphore_wait(barrier, len(place_peers) + len(z_peers) + 8 - own)

    w_z = Push(wzs, wzr)
    for peer in z_peers:
        w_z.start(zsrc, zbuf.at[z], peer)
    f_p = Push(fps, fpr)
    f_p.start(fsrc, fpair.at[zhi], z_partner)

    loads["basis"].wait()

    def compress(g, slot, l, rows):
        coded = dot(rows, V[...], 0, 0).astype(BF16)
        send1[g, :, slot, l] = coded.reshape(8, 32, RANK)

    def ex1_copy(g, n):
        return remote(
            send1.at[g, to_index[n]],
            recv1.at[g, chan],
            s1s.at[g, n],
            s1r.at[g, chan],
            to_devices[n],
        )

    def ex1_start(g):
        def row(l, carry):
            i = g * 4 + l
            cot_s[i, 0:SEG] = cot_ref[i]
            compress(g, 1, l, cot_s[i])
            values = lat_ref[i].astype(F32)
            centred = values - jnp.mean(values, axis=-1, keepdims=True)
            spread = jnp.mean(centred * centred, axis=-1, keepdims=True)
            normed_s[i, 0:SEG] = (centred * lax.rsqrt(spread + 1e-05) * gain_ref[...]).astype(BF16)
            compress(g, 0, l, normed_s[i])
            return carry

        lax.fori_loop(0, 4, row, 0)
        for n in range(8):

            @pl.when(jnp.logical_not(same(to_devices[n])))
            def _():
                ex1_copy(g, n).start()

        @pl.when(x == zlo)
        def _():
            recv1[g, chan] = send1[g, z]

    def ex1_wait(g):
        for i in range(8):

            @pl.when(jnp.logical_not(same(from_devices[i])))
            def _():
                remote(
                    send1.at[g, i], recv1.at[g, i], s1s.at[g, i], s1r.at[g, i], from_devices[i]
                ).wait_recv()

    def ex1_sent(g):
        for n in range(8):

            @pl.when(jnp.logical_not(same(to_devices[n])))
            def _():
                ex1_copy(g, n).wait_send()

    ex1_start(0)
    w_z.wait_recv()
    pk[0] = jnp.concatenate([zbuf[i, 0:4] for i in range(8)], axis=0).astype(BF16)
    pk[1] = jnp.concatenate([zbuf[i, 4:8] for i in range(8)], axis=0).astype(BF16)
    wfull[core, xy] = pk[...]
    w_x = Push(wxs, wxr)
    for peer in xy_peers:
        w_x.start(pk, wfull.at[core, xy], peer)
    f_p.wait_recv()
    fall[x] = fpair[...]
    f_a = Push(fas, far)
    for peer in x_peers:
        f_a.start(fpair, fall.at[x], peer)
    ex1_start(1)
    ex1_start(2)

    w_x.wait_recv()
    w_c = Push(wcs, wcr)
    w_c.start(wfull.at[core], wfull.at[core], sibling)
    cm_s[...] = jnp.zeros_like(cm_s)
    dc_s[...] = jnp.zeros_like(dc_s)
    gacc[...] = jnp.zeros_like(gacc)
    w_c.wait_recv()

    def mlp_step(i, carry):
        t, h = i // 4, lax.rem(i, 4)
        half, part = h // 2, pl.ds(lax.rem(h, 2) * 8, 8)
        rows = pl.ds(t * 4, 4)
        tokens = normed_s[rows].reshape(4 * PAD, 256)
        grads = cot_s[rows].reshape(4 * PAD, 256)
        w_in = wfull[half, part, 0].reshape(256, 256)
        w_out = wfull[half, part, 1].reshape(256, 256)
        value, slope = gelu_parts(dot(tokens, w_in, 1, 1))
        hidden = value.astype(BF16)
        d_pre = (dot(grads, w_out, 1, 1) * slope).astype(BF16)
        cm_s[rows] += dot(hidden, w_out).reshape(4, PAD, 256)
        dc_s[rows] += dot(d_pre, w_in).reshape(4, PAD, 256)
        gacc[half, part, 0] += dot(d_pre, tokens, 0, 0).reshape(8, 32, 256)
        gacc[half, part, 1] += dot(hidden, grads, 0, 0).reshape(8, 32, 256)
        return carry

    row = lax.broadcasted_iota(jnp.int32, (768, 1), 0)
    weight = jnp.where((row == 0) | (row == 12), 1.0, 2.0).astype(F32)

    def pair_rows(modes):
        both = [modes[:, :128].reshape(32, 24, 128), modes[:, 128:].reshape(32, 24, 128)]
        return jnp.concatenate(both, axis=1).astype(BF16)

    def split_rows(ref, g):
        both = ref[g].astype(F32)
        return both[:, :24].reshape(768, 128), both[:, 24:].reshape(768, 128)

    def swap(send, recv, send_sem, recv_sem, g):
        push = Push(send_sem.at[g], recv_sem.at[g])
        for index, peer in zip(place_index, place_peers):
            push.start(send.at[g, index], recv.at[g, place], peer)
        recv[g, place] = send[g, place]
        return push

    def zonal(g):
        ex1_wait(g)
        coded = jnp.concatenate([recv1[g, i].reshape(256, RANK) for i in range(8)], axis=1)
        modes = dot(expand[...], coded, 1, 1)
        modes = jnp.concatenate([modes[:, :128], modes[:, 128:] * weight], axis=1)
        send2[g] = pair_rows(modes)
        return swap(send2, recv2, s2s, s2r, g)

    loads["expand"].wait()
    ex2 = [None] * 3
    lax.fori_loop(0, 2, mlp_step, 0)
    ex2[0] = zonal(0)
    lax.fori_loop(2, 7, mlp_step, 0)
    ex2[1] = zonal(1)
    lax.fori_loop(7, 12, mlp_step, 0)
    gsc[...] = gacc[1 - core].astype(BF16)
    g_c = Push(gcs, gcr)
    g_c.start(gsc, grc, sibling)
    ex2[2] = zonal(2)

    r128 = lax.broadcasted_iota(jnp.int32, (128, 128), 0) // 32
    c128 = lax.broadcasted_iota(jnp.int32, (128, 128), 1) // 32
    block = (r128 == c128).astype(F32)
    lane_group = lax.broadcasted_iota(jnp.int32, (32, 128), 1) // 32

    def over_groups(tile):
        tile = tile + pltpu.roll(tile, 64, 1)
        return tile + pltpu.roll(tile, 32, 1)

    f_a.wait_recv()
    filters = fall[z // 2, lax.rem(z, 2)]

    def spread_filter(n):
        parts = []
        for part in range(2):
            w = over_groups(jnp.where(lane_group == 2 * n + part, filters, 0.0))
            parts.append(jnp.concatenate([w] * 4, axis=0) * block)
        re, im = parts
        top = jnp.concatenate([re, im], axis=1)
        low = jnp.concatenate([-im, re], axis=1)
        return jnp.concatenate([top, low], axis=0).astype(BF16)

    filter_1 = spread_filter(0)
    filter_2 = spread_filter(1)
    for name in ("first", "first_t", "second", "second_t", "tw_re", "tw_im"):
        loads[name].wait()

    def meridian_first(g):
        ex2[g].wait_recv()
        lanes = slice(g * 128, g * 128 + 128)
        modes = jnp.concatenate(split_rows(recv2, g), axis=1).astype(BF16)
        out = dot(first[...], modes)
        for slot in range(2):
            re = out[:384, slot * 128 : slot * 128 + 128]
            im = out[384:, slot * 128 : slot * 128 + 128]
            mixed_s[slot, :, lanes] = (re * tw_re[:, lanes] - im * tw_im[:, lanes]).astype(BF16)
            mixed_s[slot, :, 384 + g * 128 : 512 + g * 128] = (
                re * tw_im[:, lanes] + im * tw_re[:, lanes]
            ).astype(BF16)

    def meridian_second(slot):
        out = dot(mixed_s[slot], second[...])
        return jnp.concatenate(
            [
                jnp.concatenate(
                    [out[:, g * 128 : g * 128 + 128], out[:, 384 + g * 128 : 512 + g * 128]], axis=1
                )
                for g in range(3)
            ],
            axis=0,
        )

    def meridian_back(spectra):
        spectra = jnp.concatenate(
            [spectra[g * 384 : g * 384 + 384, :128] for g in range(3)]
            + [spectra[g * 384 : g * 384 + 384, 128:] for g in range(3)],
            axis=1,
        )
        out = dot(spectra, second_t[...])
        re, im = out[:, :384], out[:, 384:]
        h_re = re * tw_re[...] + im * tw_im[...]
        h_im = im * tw_re[...] - re * tw_im[...]
        return jnp.concatenate([h_re, h_im], axis=0).astype(BF16)

    meridian_first(0)
    meridian_first(1)

    g_c.wait_recv()
    gsx[...] = (gacc[core] + grc[...].astype(F32)).astype(BF16)
    g_x = Push(gxs, gxr)
    for index, peer in zip(xy_index, xy_peers):
        g_x.start(gsx.at[index], grx.at[xy], peer)
    grx[xy] = gsx[xy]

    meridian_first(2)
    spectrum = meridian_second(0).astype(BF16)
    value, slope = gelu_parts(dot(spectrum, filter_1))
    first_hidden = value.astype(BF16)
    second_act = dot(first_hidden, filter_2)
    bend = jnp.tanh(second_act * 10.0)
    shrunk = (second_act - 0.1 * bend).astype(BF16)
    d_second = (meridian_second(1) * bend * bend).astype(BF16)
    d_first = (dot(d_second, filter_2, 1, 1) * slope).astype(BF16)
    d_spectrum = dot(d_first, filter_1, 1, 1).astype(BF16)
    back_0 = meridian_back(shrunk)
    back_1 = meridian_back(d_spectrum)
    ex3 = []
    for g in range(3):
        lanes = slice(g * 128, g * 128 + 128)
        both = jnp.concatenate([back_0[:, lanes], back_1[:, lanes]], axis=1)
        send3[g] = pair_rows(dot(first_t[...], both))
        ex3.append(swap(send3, recv3, s3s, s3r, g))

    def fold(outer):
        o = {}
        for p in range(2):
            for q in range(2):
                tile = outer[p * 128 : p * 128 + 128, q * 128 : q * 128 + 128] * block
                o[p, q] = over_groups(tile[0:32] + tile[32:64] + tile[64:96] + tile[96:128])
        return o[0, 0] + o[1, 1], o[0, 1] - o[1, 0]

    f1_re, f1_im = fold(dot(spectrum, d_first, 0, 0))
    f2_re, f2_im = fold(dot(first_hidden, d_second, 0, 0))
    fbuf[0] = jnp.where(
        lane_group == 0, f1_re, jnp.where(lane_group == 1, f1_im, jnp.where(lane_group == 2, f2_re, f2_im))
    )
    f_c = Push(fcs, fcr)
    f_c.start(fbuf.at[0], frc, sibling)

    def unzonal(g):
        ex3[g].wait_recv()
        modes_0, modes_1 = split_rows(recv3, g)
        modes = jnp.concatenate([modes_0 * weight, modes_1], axis=1).astype(BF16)
        coded = dot(modes, expand[...], 0, 0).astype(BF16)
        for i in range(8):
            send4[g, i // 2, i % 2] = coded[:, i * RANK : i * RANK + RANK].reshape(2, 4, 32, RANK)
        push = Push(s4s.at[g], s4r.at[g])
        for index, peer in zip(x_index, x_peers):
            push.start(send4.at[g, index], mid4.at[g, x], peer)
        mid4[g, x] = send4[g, x]
        onward(g, 0)
        return push

    def ex5_copy(g, d, h):
        xs = lax.rem(x + (0, 3, 2, 1)[d], 4)
        to = h * 4 + xs
        copy = remote(
            mid4.at[g, xs, h],
            recv4.at[g, z],
            s5s.at[g, d * 2 + h],
            s5r.at[g, z],
            device(x, y, to, core),
        )
        return copy, to, xs

    def onward(g, d):
        for h in range(2):
            copy, to, xs = ex5_copy(g, d, h)

            @pl.when(to != z)
            def _():
                copy.start()

            @pl.when(to == z)
            def _():
                recv4[g, z] = mid4[g, xs, h]

    def forward(g):
        for d in range(1, 4):
            ex4[g].copies[d - 1].wait_recv()
            onward(g, d)

    def ex5_wait(g):
        for i in z_index:
            remote(
                mid4.at[g, 0, 0], recv4.at[g, i], s5s.at[g, 0], s5r.at[g, i], device(x, y, i, core)
            ).wait_recv()

    ex4 = [None] * 3
    ex4[0] = unzonal(0)
    f_c.wait_recv()
    fbuf[1] = fbuf[0] + frc[...]
    f_x = Push(fxs, fxr)
    for peer in xy_peers:
        f_x.start(fbuf.at[1], frx.at[xy], peer)
    frx[xy] = fbuf[1]
    ex4[1] = unzonal(1)
    forward(0)
    ex4[2] = unzonal(2)
    forward(1)

    g_x.wait_recv()
    summed = grx[0].astype(F32)
    for i in range(1, 16):
        summed = summed + grx[i].astype(F32)
    for i in range(8):
        gsz[i, 0:4] = summed[0, i * 4 : i * 4 + 4]
        gsz[i, 4:8] = summed[1, i * 4 : i * 4 + 4]
    g_z = Push(gzs, gzr)
    for index, peer in zip(z_index, z_peers):
        g_z.start(gsz.at[index], grz.at[z], peer)
    grz[z] = gsz[z]
    f_x.wait_recv()
    total = frx[0]
    for i in range(1, 16):
        total = total + frx[i]
    fbuf[2] = total
    f_z = Push(fzs, fzr)
    for peer in z_peers:
        f_z.start(fbuf.at[2], frz.at[z], peer)
    frz[z] = fbuf[2]
    forward(2)

    g_z.wait_recv()
    total = grz[0]
    for i in range(1, 8):
        total = total + grz[i]
    gwi_ref[...] = total[0:4]
    gwo_ref[...] = total[4:8]
    f_z.wait_recv()
    total = frz[chan]
    gff_ref[0] = total[:, 0:32]
    gff_ref[1] = total[:, 32:64]
    gfs_ref[0] = total[:, 64:96]
    gfs_ref[1] = total[:, 96:128]

    def finish(g):
        ex5_wait(g)

        def out_row(l, carry):
            i = g * 4 + l
            values = lat_ref[i].astype(F32)
            coded = recv4[g, :, 0, l].reshape(256, RANK)
            spatial = dot(V[...], coded, 1, 1)[:SEG]
            bo_ref[i] = (values + spatial + cm_s[i, 0:SEG]).astype(BF16)
            coded = recv4[g, :, 1, l].reshape(256, RANK)
            d_normed = dot(V[...], coded, 1, 1)[:SEG] + dc_s[i, 0:SEG]
            centred = values - jnp.mean(values, axis=-1, keepdims=True)
            spread = jnp.mean(centred * centred, axis=-1, keepdims=True)
            scale = lax.rsqrt(spread + 1e-05)
            unit = centred * scale
            d_unit = d_normed * gain_ref[...]
            mean_d = jnp.mean(d_unit, axis=-1, keepdims=True)
            mean_du = jnp.mean(d_unit * unit, axis=-1, keepdims=True)
            d_values = scale * (d_unit - mean_d - unit * mean_du)
            gl_ref[i] = (cot_ref[i].astype(F32) + d_values).astype(BF16)
            return carry

        lax.fori_loop(0, 4, out_row, 0)

    for g in range(3):
        finish(g)

    for push in [w_z, w_x, w_c, g_c, g_x, g_z, f_p, f_a, f_c, f_x, f_z] + ex2 + ex3 + ex4:
        push.wait_send()
    for g in range(3):
        ex1_sent(g)
        for d in range(4):
            for h in range(2):
                copy, to, xs = ex5_copy(g, d, h)

                @pl.when(to != z)
                def _():
                    copy.wait_send()


def body(latents, norm_gain, weight_in, weight_out, filter_first, filter_second, cotangent):
    table = tables()
    consts = [jnp.asarray(table[name]) for name in CONSTS]
    dma = pltpu.SemaphoreType.DMA
    vmem = pl.BlockSpec(memory_space=pltpu.VMEM)
    scratch = [pltpu.VMEM(c.shape, c.dtype) for c in consts]
    scratch += [
        pltpu.VMEM((LAT, PAD, 256), BF16),
        pltpu.VMEM((LAT, PAD, 256), BF16),
        pltpu.VMEM((3, 8, 2, 4, 32, RANK), BF16),
        pltpu.VMEM((3, 8, 2, 4, 32, RANK), BF16),
        pltpu.VMEM((3, 32, 48, 128), BF16),
        pltpu.VMEM((3, 32, 48, 128), BF16),
        pltpu.VMEM((3, 32, 48, 128), BF16),
        pltpu.VMEM((3, 32, 48, 128), BF16),
        pltpu.VMEM((3, 4, 2, 2, 4, 32, RANK), BF16),
        pltpu.VMEM((3, 4, 2, 2, 4, 32, RANK), BF16),
        pltpu.VMEM((3, 8, 2, 4, 32, RANK), BF16),
        pltpu.VMEM((2, 384, 768), BF16),
        pltpu.VMEM((LAT, PAD, 256), F32),
        pltpu.VMEM((LAT, PAD, 256), F32),
        pltpu.VMEM((8, 256), F32),
        pltpu.VMEM((8, 8, 256), F32),
        pltpu.VMEM((2, 32, 256), BF16),
        pltpu.VMEM((2, 16, 2, 32, 256), BF16),
        pltpu.VMEM((2, 16, 2, 32, 256), F32),
        pltpu.VMEM((16, 2, 32, 256), BF16),
        pltpu.VMEM((16, 2, 32, 256), BF16),
        pltpu.VMEM((16, 2, 32, 256), BF16),
        pltpu.VMEM((16, 2, 32, 256), BF16),
        pltpu.VMEM((8, 8, 256), F32),
        pltpu.VMEM((8, 8, 256), F32),
        pltpu.VMEM((32, 128), F32),
        pltpu.VMEM((2, 32, 128), F32),
        pltpu.VMEM((4, 2, 32, 128), F32),
        pltpu.VMEM((3, 32, 128), F32),
        pltpu.VMEM((32, 128), F32),
        pltpu.VMEM((16, 32, 128), F32),
        pltpu.VMEM((8, 32, 128), F32),
    ]
    scratch += [dma((len(CONSTS),))]
    for n in (8, 31, 31, 3, 8):
        scratch += [dma((3, n)), dma((3, n))]
    for n in (7, 15, 1, 7, 15, 1, 1, 3, 1, 15, 7):
        scratch += [dma((n,)), dma((n,))]
    out_shape = (
        jax.ShapeDtypeStruct(latents.shape, BF16),
        jax.ShapeDtypeStruct(latents.shape, BF16),
        jax.ShapeDtypeStruct((4, 256), F32),
        jax.ShapeDtypeStruct((4, 256), F32),
        jax.ShapeDtypeStruct((2, 32, 32), F32),
        jax.ShapeDtypeStruct((2, 32, 32), F32),
    )
    outs = pl.pallas_call(
        kernel,
        out_shape=out_shape,
        in_specs=[vmem] * 7 + [pl.BlockSpec(memory_space=pl.ANY)] * len(CONSTS),
        out_specs=(vmem,) * 6,
        scratch_shapes=scratch,
        compiler_params=pltpu.CompilerParams(
            collective_id=0, has_side_effects=True, vmem_limit_bytes=62 * 1024 * 1024
        ),
        name="spectral_block",
    )(
        latents,
        norm_gain.reshape(1, 256),
        weight_in,
        weight_out,
        filter_first.reshape(2, 32, 32),
        filter_second.reshape(2, 32, 32),
        cotangent,
        *consts,
    )
    return outs[:4] + (outs[4].reshape(2, 1, 32, 32), outs[5].reshape(2, 1, 32, 32))


def solution(mesh):
    placed = (
        P("pen", "chan", None),
        P(),
        P(("pen", "chan"), None),
        P(("pen", "chan"), None),
        P(None, "chan", None, None),
        P(None, "chan", None, None),
        P("pen", "chan", None),
    )
    return jax.shard_map(
        body,
        mesh=mesh,
        in_specs=placed,
        out_specs=(
            P("pen", "chan", None),
            P("pen", "chan", None),
            P(("pen", "chan"), None),
            P(("pen", "chan"), None),
            P(None, "chan", None, None),
            P(None, "chan", None, None),
        ),
        check_vma=False,
    )
```

time: 169 us -> 143 us (0.85); the launches traced: 169 us -> 140 us
  Pallas kernels: 162 us -> 133 us
    pallas_call x1, Pallas kernels: 162 us -> 133 us  [body(): pl.pallas_call(kernel, out_shape=out_shape, in_specs=[vmem] * 7 + [pl.Blo...]
where the time goes in v2:
time: 143 us; the launch traced here: 140 us
  Pallas kernels  133 us (93%)
  local copies, waits for them, and re-layouts  5.85 us (4%)
    pallas_call x1, Pallas kernels, body(): pl.pallas_call(kernel, out_shape=out_shape, in_specs=[vmem] * 7 + [pl.Blo...  133 us
    unnamed x16, local copies, waits for them, and re-layouts  5.85 us

profile of v2, /device:TPU:1, one launch (start us, length us, event | category | flops | bytes accessed | tf_op | source)
XLA Modules:
  0.0 139.9 jit_solution(5406395519822932782)
XLA Ops:
  0.6 133.4 %spectral_block.1 = (bf16[12,180,256]{2,1,0:T(8,128)(2,1)}, bf16[12,180,256]{2,1,0:T(8,128)(2,1)}, f32[4,256]{1,0:T(4,128)}, f32[4,256]{1,0:T(4,128)}, f32[2,32,32]{2,1,0:T(8,128)}, /*index=5*/f32[2,32,32]{2,1,0:T(8,128)}) custom-call(bf16[12,180,256]{2,1,0:T(8,128)(2,1)} %refs_0_.1, f32[1,256]{1,0:T(1,128)} %bitcast.13, bf16[4,256]{1,0:T(4,128)(2,1)} %refs_2_.1, ...), custom_call_target="tpu_custom_call" | custom-call | tf_op jit(solution)/shard_map/spectral_block/pallas_call | solution.py:626
  134.1 0.0 copy-start
  134.1 2.4 %copy.29 = bf16[12,180,256]{2,1,0:T(8,128)(2,1)} copy(bf16[12,180,256]{2,1,0:T(8,128)(2,1)} %get-tuple-element.30) | data formatting | bytes 2211840
  136.5 0.0 copy-done
  136.5 0.0 copy-start.4
  136.5 0.0 copy-start.3
  136.5 0.0 copy-start.2
  136.5 0.0 copy-start.1
  136.5 1.0 copy.30
  137.5 0.0 copy-done.4
  137.5 0.6 copy.31
  138.1 0.0 copy-done.3
  138.1 0.6 copy.32
  138.7 0.0 copy-done.2
  138.7 0.6 copy.33
  139.3 0.0 copy-done.1
  139.3 0.6 copy.34
Async XLA Ops:
  134.1 2.4 %copy-start = (bf16[12,180,256]{2,1,0:T(8,128)(2,1)S(1)}, bf16[12,180,256]{2,1,0:T(8,128)(2,1)}, u32[]{:S(2)}) copy-start(bf16[12,180,256]{2,1,0:T(8,128)(2,1)} %get-tuple-element.31) | copy-start | bytes 3317764
  136.5 1.0 copy-start.4
  136.5 1.6 %copy-start.3 = (f32[4,256]{1,0:T(4,128)S(1)}, f32[4,256]{1,0:T(4,128)}, u32[]{:S(2)}) copy-start(f32[4,256]{1,0:T(4,128)} %get-tuple-element.33) | copy-start | bytes 12292
  136.5 2.2 %copy-start.2 = (f32[2,32,32]{2,1,0:T(8,128)S(1)}, f32[2,32,32]{2,1,0:T(8,128)}, u32[]{:S(2)}) copy-start(f32[2,32,32]{2,1,0:T(8,128)} %get-tuple-element.16) | copy-start | bytes 24580
  136.5 2.8 %copy-start.1 = (f32[2,32,32]{2,1,0:T(8,128)S(1)}, f32[2,32,32]{2,1,0:T(8,128)}, u32[]{:S(2)}) copy-start(f32[2,32,32]{2,1,0:T(8,128)} %get-tuple-element.17) | copy-start | bytes 24580

commit v3 on v2

--- a/solution.py
+++ b/solution.py
@@ -14,7 +14,7 @@
 NLON, KLON, NLAT = 1440, 384, 384
 SEG = 180
 PAD = 192
-RANK = 128
+RANK = 112
 LAT = 12
 NK = 12
 GELU_C = math.sqrt(2.0 / math.pi)
@@ -53,7 +53,9 @@
     twiddle = np.repeat(np.repeat(twiddle, NK, axis=0), 32, axis=1)
     return dict(
         basis=as_bf16(basis_pad),
+        basis_t=as_bf16(basis_pad.T),
         expand=as_bf16(expand),
+        expand_t=as_bf16(expand.T),
         first=as_bf16(first),
         first_t=as_bf16(first.T),
         second=as_bf16(second),
@@ -63,7 +65,7 @@
     )
 
 
-CONSTS = ("basis", "expand", "first", "first_t", "second", "second_t", "tw_re", "tw_im")
+CONSTS = ("basis_t", "expand", "first", "tw_re", "tw_im", "second", "second_t", "first_t", "expand_t", "basis")
 
 
 def dot(a, b, ca=1, cb=0):
@@ -110,27 +112,31 @@
 
 
 def kernel(*refs):
-    (lat_ref, gain_ref, win_ref, wout_ref, ff_ref, fs_ref, cot_ref) = refs[:7]
+    (lat_hbm, gain_ref, win_ref, wout_ref, ff_ref, fs_ref, cot_hbm) = refs[:7]
     const_hbm = refs[7 : 7 + len(CONSTS)]
     refs = refs[7 + len(CONSTS) :]
-    (bo_ref, gl_ref, gwi_ref, gwo_ref, gff_ref, gfs_ref) = refs[:6]
-    refs = refs[6:]
+    (bo_hbm, gl_hbm, gwi_ref, gwo_ref, gff_ref, gfs_ref) = refs[:6]
+    (lat_ref, cot_ref, bo_ref, gl_ref, io_sem) = refs[6:11]
+    refs = refs[11:]
     const = refs[: len(CONSTS)]
     refs = refs[len(CONSTS) :]
     (normed_s, cot_s, send1, recv1, send2, recv2, send3, recv3, send4, mid4, recv4) = refs[:11]
-    (mixed_s, cm_s, dc_s, zsrc, zbuf, pk, wfull, gacc, gsc, grc, gsx, grx, gsz, grz) = refs[11:25]
+    (mixed_s, cm_s, dc_s, zsrc, zbuf, pk, wfull, gacc, gsc, grc, gsy, gry, gsx) = refs[11:24]
+    (grx, gsz, grz) = refs[24:27]
+    refs = refs[2:]
     (fsrc, fpair, fall, fbuf, frc, frx, frz) = refs[25:32]
     (const_sem, s1s, s1r, s2s, s2r, s3s, s3r, s4s, s4r, s5s, s5r) = refs[32:43]
-    (wzs, wzr, wxs, wxr, wcs, wcr, gzs, gzr, gxs, gxr, gcs, gcr) = refs[43:55]
-    (fps, fpr, fas, far, fcs, fcr, fxs, fxr, fzs, fzr) = refs[55:65]
-    V, expand, first, first_t, second, second_t, tw_re, tw_im = const
+    (wzs, wzr, wxs, wxr, wys, wyr, wcs, wcr) = refs[43:51]
+    (gzs, gzr, gxs, gxr, gys, gyr, gcs, gcr) = refs[51:59]
+    (fps, fpr, fas, far, fcs, fcr, fxs, fxr, fzs, fzr) = refs[59:69]
+    Vt, expand, first, tw_re, tw_im, second, second_t, first_t, expand_t, V = const
 
     pen = lax.axis_index("pen")
     chan = lax.axis_index("chan")
     x, zhi = chan // 2, lax.rem(chan, 2)
     y, zlo, core = pen // 8, lax.rem(pen // 2, 4), lax.rem(pen, 2)
     z = zhi * 4 + zlo
-    xy = x * 4 + y
+    xy = y * 4 + x
     place = y * 8 + x * 2 + core
 
     def device(x_, y_, z_, core_):
@@ -145,8 +151,17 @@
     z_index = [lax.rem(z + d, 8) for d in range(1, 8)]
     z_peers = [device(x, y, i, core) for i in z_index]
     xy_index = [lax.rem(xy + d, 16) for d in range(1, 16)]
-    xy_peers = [device(i // 4, lax.rem(i, 4), z, core) for i in xy_index]
-    place_index = [lax.rem(place + d, 32) for d in range(1, 32)]
+    xy_peers = [device(lax.rem(i, 4), i // 4, z, core) for i in xy_index]
+    y_index = [lax.rem(y + d, 4) for d in range(1, 4)]
+    y_peers = [device(x, i, z, core) for i in y_index]
+    order = [(2, 2), (2, 1), (2, 3), (1, 2), (3, 2), (2, 0), (0, 2), (1, 1), (3, 3), (1, 3), (3, 1)]
+    order += [(1, 0), (3, 0), (0, 1), (0, 3), (0, 0)]
+    place_index = [
+        lax.rem(y + dy, 4) * 8 + lax.rem(x + dx, 4) * 2 + lax.rem(core + dc, 2)
+        for dx, dy in order
+        for dc in (0, 1)
+        if (dx, dy, dc) != (0, 0, 0)
+    ]
     place_peers = [member(p) for p in place_index]
     sibling = device(x, y, z, 1 - core)
     x_index = [lax.rem(x + d, 4) for d in range(1, 4)]
@@ -156,6 +171,12 @@
     to_devices = [device(zlo, y, i, core) for i in to_index]
     from_devices = [device(i // 2, y, (i % 2) * 4 + x, core) for i in range(8)]
 
+    reads = []
+    for g in range(3):
+        part = pl.ds(g * 4, 4)
+        for n, (src, dst) in enumerate(((lat_hbm, lat_ref), (cot_hbm, cot_ref))):
+            reads.append(pltpu.make_async_copy(src.at[part], dst.at[part], io_sem.at[g * 2 + n]))
+            reads[-1].start()
     loads = []
     for n, (src, dst) in enumerate(zip(const_hbm, const)):
         load = pltpu.make_async_copy(src, dst, const_sem.at[n])
@@ -191,11 +212,7 @@
     f_p = Push(fps, fpr)
     f_p.start(fsrc, fpair.at[zhi], z_partner)
 
-    loads["basis"].wait()
-
-    def compress(g, slot, l, rows):
-        coded = dot(rows, V[...], 0, 0).astype(BF16)
-        send1[g, :, slot, l] = coded.reshape(8, 32, RANK)
+    loads["basis_t"].wait()
 
     def ex1_copy(g, n):
         return remote(
@@ -207,18 +224,24 @@
         )
 
     def ex1_start(g):
+        reads[2 * g].wait()
+        reads[2 * g + 1].wait()
+
         def row(l, carry):
             i = g * 4 + l
             cot_s[i, 0:SEG] = cot_ref[i]
-            compress(g, 1, l, cot_s[i])
             values = lat_ref[i].astype(F32)
             centred = values - jnp.mean(values, axis=-1, keepdims=True)
             spread = jnp.mean(centred * centred, axis=-1, keepdims=True)
             normed_s[i, 0:SEG] = (centred * lax.rsqrt(spread + 1e-05) * gain_ref[...]).astype(BF16)
-            compress(g, 0, l, normed_s[i])
             return carry
 
         lax.fori_loop(0, 4, row, 0)
+        for slot, rows in enumerate((normed_s, cot_s)):
+            coded = [dot(Vt[...], rows[g * 4 + l]) for l in range(4)]
+            for b in range(8):
+                part = jnp.concatenate([c[:, 32 * b : 32 * b + 32] for c in coded], axis=1)
+                send1[g, b, slot] = part.astype(BF16)
         for n in range(8):
 
             @pl.when(jnp.logical_not(same(to_devices[n])))
@@ -251,7 +274,7 @@
     pk[1] = jnp.concatenate([zbuf[i, 4:8] for i in range(8)], axis=0).astype(BF16)
     wfull[core, xy] = pk[...]
     w_x = Push(wxs, wxr)
-    for peer in xy_peers:
+    for peer in x_peers:
         w_x.start(pk, wfull.at[core, xy], peer)
     f_p.wait_recv()
     fall[x] = fpair[...]
@@ -262,6 +285,11 @@
     ex1_start(2)
 
     w_x.wait_recv()
+    w_y = Push(wys, wyr)
+    own_y = pl.ds(y * 4, 4)
+    for peer in y_peers:
+        w_y.start(wfull.at[core, own_y], wfull.at[core, own_y], peer)
+    w_y.wait_recv()
     w_c = Push(wcs, wcr)
     w_c.start(wfull.at[core], wfull.at[core], sibling)
     cm_s[...] = jnp.zeros_like(cm_s)
@@ -306,8 +334,10 @@
 
     def zonal(g):
         ex1_wait(g)
-        coded = jnp.concatenate([recv1[g, i].reshape(256, RANK) for i in range(8)], axis=1)
-        modes = dot(expand[...], coded, 1, 1)
+        coded = jnp.concatenate(
+            [jnp.concatenate([recv1[g, i, 0], recv1[g, i, 1]], axis=1) for i in range(8)], axis=0
+        )
+        modes = dot(expand[...], coded)
         modes = jnp.concatenate([modes[:, :128], modes[:, 128:] * weight], axis=1)
         send2[g] = pair_rows(modes)
         return swap(send2, recv2, s2s, s2r, g)
@@ -348,7 +378,7 @@
 
     filter_1 = spread_filter(0)
     filter_2 = spread_filter(1)
-    for name in ("first", "first_t", "second", "second_t", "tw_re", "tw_im"):
+    for name in CONSTS[2:]:
         loads[name].wait()
 
     def meridian_first(g):
@@ -392,11 +422,11 @@
     meridian_first(1)
 
     g_c.wait_recv()
-    gsx[...] = (gacc[core] + grc[...].astype(F32)).astype(BF16)
-    g_x = Push(gxs, gxr)
-    for index, peer in zip(xy_index, xy_peers):
-        g_x.start(gsx.at[index], grx.at[xy], peer)
-    grx[xy] = gsx[xy]
+    gsy[...] = (gacc[core] + grc[...].astype(F32)).astype(BF16)
+    g_y = Push(gys, gyr)
+    for index, peer in zip(y_index, y_peers):
+        g_y.start(gsy.at[pl.ds(index * 4, 4)], gry.at[y], peer)
+    gry[y] = gsy[own_y]
 
     meridian_first(2)
     spectrum = meridian_second(0).astype(BF16)
@@ -437,9 +467,11 @@
         ex3[g].wait_recv()
         modes_0, modes_1 = split_rows(recv3, g)
         modes = jnp.concatenate([modes_0 * weight, modes_1], axis=1).astype(BF16)
-        coded = dot(modes, expand[...], 0, 0).astype(BF16)
+        coded = dot(expand_t[...], modes)
         for i in range(8):
-            send4[g, i // 2, i % 2] = coded[:, i * RANK : i * RANK + RANK].reshape(2, 4, 32, RANK)
+            for slot in range(2):
+                part = coded[i * RANK : i * RANK + RANK, slot * 128 : slot * 128 + 128]
+                send4[g, i // 2, i % 2, slot] = part.astype(BF16)
         push = Push(s4s.at[g], s4r.at[g])
         for index, peer in zip(x_index, x_peers):
             push.start(send4.at[g, index], mid4.at[g, x], peer)
@@ -490,6 +522,14 @@
     for peer in xy_peers:
         f_x.start(fbuf.at[1], frx.at[xy], peer)
     frx[xy] = fbuf[1]
+    g_y.wait_recv()
+    gsx[...] = (
+        (gry[0].astype(F32) + gry[1].astype(F32)) + (gry[2].astype(F32) + gry[3].astype(F32))
+    ).astype(BF16)
+    g_x = Push(gxs, gxr)
+    for index, peer in zip(x_index, x_peers):
+        g_x.start(gsx.at[index], grx.at[x], peer)
+    grx[x] = gsx[x]
     ex4[1] = unzonal(1)
     forward(0)
     ex4[2] = unzonal(2)
@@ -497,7 +537,7 @@
 
     g_x.wait_recv()
     summed = grx[0].astype(F32)
-    for i in range(1, 16):
+    for i in range(1, 4):
         summed = summed + grx[i].astype(F32)
     for i in range(8):
         gsz[i, 0:4] = summed[0, i * 4 : i * 4 + 4]
@@ -530,17 +570,20 @@
     gfs_ref[0] = total[:, 64:96]
     gfs_ref[1] = total[:, 96:128]
 
+    writes = []
+
     def finish(g):
         ex5_wait(g)
 
-        def out_row(l, carry):
+        for l in range(4):
             i = g * 4 + l
+            lanes = slice(32 * l, 32 * l + 32)
             values = lat_ref[i].astype(F32)
-            coded = recv4[g, :, 0, l].reshape(256, RANK)
-            spatial = dot(V[...], coded, 1, 1)[:SEG]
+            coded = jnp.concatenate([recv4[g, b, 0][:, lanes] for b in range(8)], axis=1)
+            spatial = dot(V[...], coded)[:SEG]
             bo_ref[i] = (values + spatial + cm_s[i, 0:SEG]).astype(BF16)
-            coded = recv4[g, :, 1, l].reshape(256, RANK)
-            d_normed = dot(V[...], coded, 1, 1)[:SEG] + dc_s[i, 0:SEG]
+            coded = jnp.concatenate([recv4[g, b, 1][:, lanes] for b in range(8)], axis=1)
+            d_normed = dot(V[...], coded)[:SEG] + dc_s[i, 0:SEG]
             centred = values - jnp.mean(values, axis=-1, keepdims=True)
             spread = jnp.mean(centred * centred, axis=-1, keepdims=True)
             scale = lax.rsqrt(spread + 1e-05)
@@ -550,14 +593,18 @@
             mean_du = jnp.mean(d_unit * unit, axis=-1, keepdims=True)
             d_values = scale * (d_unit - mean_d - unit * mean_du)
             gl_ref[i] = (cot_ref[i].astype(F32) + d_values).astype(BF16)
-            return carry
-
-        lax.fori_loop(0, 4, out_row, 0)
+        part = pl.ds(g * 4, 4)
+        for n, (src, dst) in enumerate(((bo_ref, bo_hbm), (gl_ref, gl_hbm))):
+            write = pltpu.make_async_copy(src.at[part], dst.at[part], io_sem.at[6 + g * 2 + n])
+            write.start()
+            writes.append(write)
 
     for g in range(3):
         finish(g)
 
-    for push in [w_z, w_x, w_c, g_c, g_x, g_z, f_p, f_a, f_c, f_x, f_z] + ex2 + ex3 + ex4:
+    for write in writes:
+        write.wait()
+    for push in [w_z, w_x, w_y, w_c, g_c, g_y, g_x, g_z, f_p, f_a, f_c, f_x, f_z] + ex2 + ex3 + ex4:
         push.wait_send()
     for g in range(3):
         ex1_sent(g)
@@ -575,19 +622,21 @@
     consts = [jnp.asarray(table[name]) for name in CONSTS]
     dma = pltpu.SemaphoreType.DMA
     vmem = pl.BlockSpec(memory_space=pltpu.VMEM)
-    scratch = [pltpu.VMEM(c.shape, c.dtype) for c in consts]
+    hbm = pl.BlockSpec(memory_space=pl.ANY)
+    scratch = [pltpu.VMEM(latents.shape, BF16)] * 4 + [dma((12,))]
+    scratch += [pltpu.VMEM(c.shape, c.dtype) for c in consts]
     scratch += [
         pltpu.VMEM((LAT, PAD, 256), BF16),
         pltpu.VMEM((LAT, PAD, 256), BF16),
-        pltpu.VMEM((3, 8, 2, 4, 32, RANK), BF16),
-        pltpu.VMEM((3, 8, 2, 4, 32, RANK), BF16),
+        pltpu.VMEM((3, 8, 2, RANK, 128), BF16),
+        pltpu.VMEM((3, 8, 2, RANK, 128), BF16),
         pltpu.VMEM((3, 32, 48, 128), BF16),
         pltpu.VMEM((3, 32, 48, 128), BF16),
         pltpu.VMEM((3, 32, 48, 128), BF16),
         pltpu.VMEM((3, 32, 48, 128), BF16),
-        pltpu.VMEM((3, 4, 2, 2, 4, 32, RANK), BF16),
-        pltpu.VMEM((3, 4, 2, 2, 4, 32, RANK), BF16),
-        pltpu.VMEM((3, 8, 2, 4, 32, RANK), BF16),
+        pltpu.VMEM((3, 4, 2, 2, RANK, 128), BF16),
+        pltpu.VMEM((3, 4, 2, 2, RANK, 128), BF16),
+        pltpu.VMEM((3, 8, 2, RANK, 128), BF16),
         pltpu.VMEM((2, 384, 768), BF16),
         pltpu.VMEM((LAT, PAD, 256), F32),
         pltpu.VMEM((LAT, PAD, 256), F32),
@@ -599,7 +648,9 @@
         pltpu.VMEM((16, 2, 32, 256), BF16),
         pltpu.VMEM((16, 2, 32, 256), BF16),
         pltpu.VMEM((16, 2, 32, 256), BF16),
-        pltpu.VMEM((16, 2, 32, 256), BF16),
+        pltpu.VMEM((4, 4, 2, 32, 256), BF16),
+        pltpu.VMEM((4, 2, 32, 256), BF16),
+        pltpu.VMEM((4, 2, 32, 256), BF16),
         pltpu.VMEM((8, 8, 256), F32),
         pltpu.VMEM((8, 8, 256), F32),
         pltpu.VMEM((32, 128), F32),
@@ -613,7 +664,7 @@
     scratch += [dma((len(CONSTS),))]
     for n in (8, 31, 31, 3, 8):
         scratch += [dma((3, n)), dma((3, n))]
-    for n in (7, 15, 1, 7, 15, 1, 1, 3, 1, 15, 7):
+    for n in (7, 3, 3, 1, 7, 3, 3, 1, 1, 3, 1, 15, 7):
         scratch += [dma((n,)), dma((n,))]
     out_shape = (
         jax.ShapeDtypeStruct(latents.shape, BF16),
@@ -626,8 +677,8 @@
     outs = pl.pallas_call(
         kernel,
         out_shape=out_shape,
-        in_specs=[vmem] * 7 + [pl.BlockSpec(memory_space=pl.ANY)] * len(CONSTS),
-        out_specs=(vmem,) * 6,
+        in_specs=[hbm] + [vmem] * 5 + [hbm] * (1 + len(CONSTS)),
+        out_specs=(hbm,) * 2 + (vmem,) * 4,
         scratch_shapes=scratch,
         compiler_params=pltpu.CompilerParams(
             collective_id=0, has_side_effects=True, vmem_limit_bytes=62 * 1024 * 1024

time: 143 us -> 130 us (0.909); the launches traced: 140 us -> 129 us
  Pallas kernels: 133 us -> 122 us
    pallas_call x1, Pallas kernels: 133 us -> 122 us  [body(): pl.pallas_call(kernel, out_shape=out_shape, in_specs=[hbm] + [vmem] * 5 +...]
where the time goes in v3:
time: 130 us; the launch traced here: 129 us
  Pallas kernels  122 us (94%)
  local copies, waits for them, and re-layouts  5.85 us (4%)
    pallas_call x1, Pallas kernels, body(): pl.pallas_call(kernel, out_shape=out_shape, in_specs=[hbm] + [vmem] * 5 +...  122 us
    unnamed x16, local copies, waits for them, and re-layouts  5.85 us

profile of v3, /device:TPU:1, one launch (start us, length us, event | category | flops | bytes accessed | tf_op | source)
XLA Modules:
  0.0 128.7 jit_solution(1465297317215512592)
XLA Ops:
  0.6 122.2 %spectral_block.1 = (bf16[12,180,256]{2,1,0:T(8,128)(2,1)}, bf16[12,180,256]{2,1,0:T(8,128)(2,1)}, f32[4,256]{1,0:T(4,128)}, f32[4,256]{1,0:T(4,128)}, f32[2,32,32]{2,1,0:T(8,128)}, /*index=5*/f32[2,32,32]{2,1,0:T(8,128)}) custom-call(bf16[12,180,256]{2,1,0:T(8,128)(2,1)} %refs_0_.1, f32[1,256]{1,0:T(1,128)} %bitcast.13, bf16[4,256]{1,0:T(4,128)(2,1)} %refs_2_.1, ...), custom_call_target="tpu_custom_call" | custom-call | tf_op jit(solution)/shard_map/spectral_block/pallas_call | solution.py:677
  122.8 0.0 copy-start
  122.8 2.4 %copy.31 = bf16[12,180,256]{2,1,0:T(8,128)(2,1)} copy(bf16[12,180,256]{2,1,0:T(8,128)(2,1)} %get-tuple-element.30) | data formatting | bytes 2211840
  125.2 0.0 copy-done
  125.3 0.0 copy-start.4
  125.3 0.0 copy-start.3
  125.3 0.0 copy-start.2
  125.3 0.0 copy-start.1
  125.3 1.0 copy.32
  126.3 0.0 copy-done.4
  126.3 0.6 copy.33
  126.9 0.0 copy-done.3
  126.9 0.6 copy.34
  127.5 0.0 copy-done.2
  127.5 0.6 copy.35
  128.1 0.0 copy-done.1
  128.1 0.6 copy.36
Async XLA Ops:
  122.8 2.4 %copy-start = (bf16[12,180,256]{2,1,0:T(8,128)(2,1)S(1)}, bf16[12,180,256]{2,1,0:T(8,128)(2,1)}, u32[]{:S(2)}) copy-start(bf16[12,180,256]{2,1,0:T(8,128)(2,1)} %get-tuple-element.31) | copy-start | bytes 3317764
  125.3 1.0 copy-start.4
  125.3 1.6 %copy-start.3 = (f32[4,256]{1,0:T(4,128)S(1)}, f32[4,256]{1,0:T(4,128)}, u32[]{:S(2)}) copy-start(f32[4,256]{1,0:T(4,128)} %get-tuple-element.33) | copy-start | bytes 12292
  125.3 2.2 %copy-start.2 = (f32[2,32,32]{2,1,0:T(8,128)S(1)}, f32[2,32,32]{2,1,0:T(8,128)}, u32[]{:S(2)}) copy-start(f32[2,32,32]{2,1,0:T(8,128)} %get-tuple-element.16) | copy-start | bytes 24580
  125.3 2.8 %copy-start.1 = (f32[2,32,32]{2,1,0:T(8,128)S(1)}, f32[2,32,32]{2,1,0:T(8,128)}, u32[]{:S(2)}) copy-start(f32[2,32,32]{2,1,0:T(8,128)} %get-tuple-element.17) | copy-start | bytes 24580

commit v4 on v3

--- a/solution.py
+++ b/solution.py
@@ -115,9 +115,10 @@
     (lat_hbm, gain_ref, win_ref, wout_ref, ff_ref, fs_ref, cot_hbm) = refs[:7]
     const_hbm = refs[7 : 7 + len(CONSTS)]
     refs = refs[7 + len(CONSTS) :]
-    (bo_hbm, gl_hbm, gwi_ref, gwo_ref, gff_ref, gfs_ref) = refs[:6]
-    (lat_ref, cot_ref, bo_ref, gl_ref, io_sem) = refs[6:11]
-    refs = refs[11:]
+    (fields_hbm, gw_ref, gf_ref) = refs[:3]
+    bo_hbm, gl_hbm = fields_hbm.at[0], fields_hbm.at[1]
+    (lat_ref, cot_ref, bo_ref, gl_ref, io_sem) = refs[3:8]
+    refs = refs[8:]
     const = refs[: len(CONSTS)]
     refs = refs[len(CONSTS) :]
     (normed_s, cot_s, send1, recv1, send2, recv2, send3, recv3, send4, mid4, recv4) = refs[:11]
@@ -346,13 +347,14 @@
     ex2 = [None] * 3
     lax.fori_loop(0, 2, mlp_step, 0)
     ex2[0] = zonal(0)
-    lax.fori_loop(2, 7, mlp_step, 0)
+    lax.fori_loop(2, 6, mlp_step, 0)
     ex2[1] = zonal(1)
-    lax.fori_loop(7, 12, mlp_step, 0)
+    lax.fori_loop(6, 9, mlp_step, 0)
+    ex2[2] = zonal(2)
+    lax.fori_loop(9, 12, mlp_step, 0)
     gsc[...] = gacc[1 - core].astype(BF16)
     g_c = Push(gcs, gcr)
     g_c.start(gsc, grc, sibling)
-    ex2[2] = zonal(2)
 
     r128 = lax.broadcasted_iota(jnp.int32, (128, 128), 0) // 32
     c128 = lax.broadcasted_iota(jnp.int32, (128, 128), 1) // 32
@@ -420,13 +422,6 @@
 
     meridian_first(0)
     meridian_first(1)
-
-    g_c.wait_recv()
-    gsy[...] = (gacc[core] + grc[...].astype(F32)).astype(BF16)
-    g_y = Push(gys, gyr)
-    for index, peer in zip(y_index, y_peers):
-        g_y.start(gsy.at[pl.ds(index * 4, 4)], gry.at[y], peer)
-    gry[y] = gsy[own_y]
 
     meridian_first(2)
     spectrum = meridian_second(0).astype(BF16)
@@ -515,13 +510,24 @@
             ).wait_recv()
 
     ex4 = [None] * 3
+    g_c.wait_recv()
+    gsy[...] = (gacc[core] + grc[...].astype(F32)).astype(BF16)
+    g_y = Push(gys, gyr)
+    for index, peer in zip(y_index, y_peers):
+        g_y.start(gsy.at[pl.ds(index * 4, 4)], gry.at[y], peer)
+    gry[y] = gsy[own_y]
+
     ex4[0] = unzonal(0)
+    ex4[1] = unzonal(1)
+    forward(0)
+    ex4[2] = unzonal(2)
     f_c.wait_recv()
     fbuf[1] = fbuf[0] + frc[...]
     f_x = Push(fxs, fxr)
     for peer in xy_peers:
         f_x.start(fbuf.at[1], frx.at[xy], peer)
     frx[xy] = fbuf[1]
+
     g_y.wait_recv()
     gsx[...] = (
         (gry[0].astype(F32) + gry[1].astype(F32)) + (gry[2].astype(F32) + gry[3].astype(F32))
@@ -530,10 +536,9 @@
     for index, peer in zip(x_index, x_peers):
         g_x.start(gsx.at[index], grx.at[x], peer)
     grx[x] = gsx[x]
-    ex4[1] = unzonal(1)
-    forward(0)
-    ex4[2] = unzonal(2)
+
     forward(1)
+    forward(2)
 
     g_x.wait_recv()
     summed = grx[0].astype(F32)
@@ -546,6 +551,7 @@
     for index, peer in zip(z_index, z_peers):
         g_z.start(gsz.at[index], grz.at[z], peer)
     grz[z] = gsz[z]
+
     f_x.wait_recv()
     total = frx[0]
     for i in range(1, 16):
@@ -555,20 +561,6 @@
     for peer in z_peers:
         f_z.start(fbuf.at[2], frz.at[z], peer)
     frz[z] = fbuf[2]
-    forward(2)
-
-    g_z.wait_recv()
-    total = grz[0]
-    for i in range(1, 8):
-        total = total + grz[i]
-    gwi_ref[...] = total[0:4]
-    gwo_ref[...] = total[4:8]
-    f_z.wait_recv()
-    total = frz[chan]
-    gff_ref[0] = total[:, 0:32]
-    gff_ref[1] = total[:, 32:64]
-    gfs_ref[0] = total[:, 64:96]
-    gfs_ref[1] = total[:, 96:128]
 
     writes = []
 
@@ -599,8 +591,22 @@
             write.start()
             writes.append(write)
 
-    for g in range(3):
-        finish(g)
+    finish(0)
+    finish(1)
+    g_z.wait_recv()
+    total = grz[0]
+    for i in range(1, 8):
+        total = total + grz[i]
+    gw_ref[0] = total[0:4]
+    gw_ref[1] = total[4:8]
+    f_z.wait_recv()
+    total = frz[chan]
+    for n in range(2):
+        for part in range(2):
+            lo = n * 64 + part * 32
+            gf_ref[n, part] = total[:, lo : lo + 32]
+
+    finish(2)
 
     for write in writes:
         write.wait()
@@ -667,18 +673,15 @@
     for n in (7, 3, 3, 1, 7, 3, 3, 1, 1, 3, 1, 15, 7):
         scratch += [dma((n,)), dma((n,))]
     out_shape = (
-        jax.ShapeDtypeStruct(latents.shape, BF16),
-        jax.ShapeDtypeStruct(latents.shape, BF16),
-        jax.ShapeDtypeStruct((4, 256), F32),
-        jax.ShapeDtypeStruct((4, 256), F32),
-        jax.ShapeDtypeStruct((2, 32, 32), F32),
-        jax.ShapeDtypeStruct((2, 32, 32), F32),
+        jax.ShapeDtypeStruct((2,) + latents.shape, BF16),
+        jax.ShapeDtypeStruct((2, 4, 256), F32),
+        jax.ShapeDtypeStruct((2, 2, 32, 32), F32),
     )
     outs = pl.pallas_call(
         kernel,
         out_shape=out_shape,
         in_specs=[hbm] + [vmem] * 5 + [hbm] * (1 + len(CONSTS)),
-        out_specs=(hbm,) * 2 + (vmem,) * 4,
+        out_specs=(hbm,) + (vmem,) * 2,
         scratch_shapes=scratch,
         compiler_params=pltpu.CompilerParams(
             collective_id=0, has_side_effects=True, vmem_limit_bytes=62 * 1024 * 1024
@@ -694,7 +697,9 @@
         cotangent,
         *consts,
     )
-    return outs[:4] + (outs[4].reshape(2, 1, 32, 32), outs[5].reshape(2, 1, 32, 32))
+    fields, weights, filters = outs
+    filters = filters.reshape(2, 2, 1, 32, 32)
+    return fields[0], fields[1], weights[0], weights[1], filters[0], filters[1]
 
 
 def solution(mesh):

time: 130 us -> 127 us (0.977)
  local copies, waits for them, and re-layouts: 5.85 us -> 4.38 us
    unnamed x16 -> x5, local copies, waits for them, and re-layouts: 5.85 us -> 0.64 us
    squeeze x0 -> x2, local copies, waits for them, and re-layouts: none -> 3.74 us  [the longest x1 3.14 us: body(): fields[1]]
where the time goes in v4:
time: 127 us
  Pallas kernels  122 us (96%)
  local copies, waits for them, and re-layouts  4.38 us (3%)
    pallas_call x1, Pallas kernels, body(): pl.pallas_call(kernel, out_shape=out_shape, in_specs=[hbm] + [vmem] * 5 +...  122 us
    squeeze x1, local copies, waits for them, and re-layouts, body(): fields[1]  3.14 us

profile of v4, /device:TPU:1, one launch (start us, length us, event | category | flops | bytes accessed | tf_op | source)
XLA Modules:
  0.0 126.8 jit_solution(9478116452251579911)
XLA Ops:
  0.6 121.7 %spectral_block.1 = (bf16[2,12,180,256]{3,2,1,0:T(8,128)(2,1)}, f32[2,4,256]{2,1,0:T(4,128)}, f32[2,2,32,32]{3,2,1,0:T(8,128)}) custom-call(bf16[12,180,256]{2,1,0:T(8,128)(2,1)} %refs_0_.1, f32[1,256]{1,0:T(1,128)} %bitcast.21, bf16[4,256]{1,0:T(4,128)(2,1)} %refs_2_.1, bf16[4,256]{1,0:T(4,128)(2,1)} %refs_3_.1, bf16[2,32,32]{2,1,0:T(8,128)(2,1)} %bitcast.19, ...), custom_call_target="tpu_custom_call" | custom-call | tf_op jit(solution)/shard_map/spectral_block/pallas_call | solution.py:680
  122.4 0.0 copy-start.1
  122.4 0.0 copy-start
  122.4 3.1 %slice_bitcast_fusion = (bf16[12,180,256]{2,1,0:T(8,128)(2,1)}, bf16[12,180,256]{2,1,0:T(8,128)(2,1)}) fusion(bf16[2,12,180,256]{3,2,1,0:T(8,128)(2,1)} %get-tuple-element.9), kind=kLoop, calls=%fused_computation | loop fusion | bytes 4423680 | tf_op jit(solution)/shard_map/squeeze | solution.py:702
  125.6 0.0 copy-done.1
  125.6 0.6 slice_bitcast_fusion.4
  126.2 0.0 copy-done
  126.2 0.6 slice_bitcast_fusion.2
Async XLA Ops:
  122.4 3.2 %copy-start.1 = (f32[2,4,256]{2,1,0:T(4,128)S(1)}, f32[2,4,256]{2,1,0:T(4,128)}, u32[]{:S(2)}) copy-start(f32[2,4,256]{2,1,0:T(4,128)} %get-tuple-element.10) | copy-start | bytes 24580
  122.4 3.8 %copy-start = (f32[2,2,32,32]{3,2,1,0:T(8,128)S(1)}, f32[2,2,32,32]{3,2,1,0:T(8,128)}, u32[]{:S(2)}) copy-start(f32[2,2,32,32]{3,2,1,0:T(8,128)} %get-tuple-element.11) | copy-start | bytes 49156

commit v5 on v4

--- a/solution.py
+++ b/solution.py
@@ -178,21 +178,21 @@
         for n, (src, dst) in enumerate(((lat_hbm, lat_ref), (cot_hbm, cot_ref))):
             reads.append(pltpu.make_async_copy(src.at[part], dst.at[part], io_sem.at[g * 2 + n]))
             reads[-1].start()
+    barrier = pltpu.get_barrier_semaphore()
+    for peer in place_peers + z_peers:
+        pl.semaphore_signal(barrier, inc=1, device_id=peer, device_id_type=MESH)
+    for peer in from_devices:
+
+        @pl.when(jnp.logical_not(same(peer)))
+        def _():
+            pl.semaphore_signal(barrier, inc=1, device_id=peer, device_id_type=MESH)
+
     loads = []
     for n, (src, dst) in enumerate(zip(const_hbm, const)):
         load = pltpu.make_async_copy(src, dst, const_sem.at[n])
         load.start()
         loads.append(load)
     loads = dict(zip(CONSTS, loads))
-
-    barrier = pltpu.get_barrier_semaphore()
-    for peer in place_peers + z_peers:
-        pl.semaphore_signal(barrier, inc=1, device_id=peer, device_id_type=MESH)
-    for peer in from_devices:
-
-        @pl.when(jnp.logical_not(same(peer)))
-        def _():
-            pl.semaphore_signal(barrier, inc=1, device_id=peer, device_id_type=MESH)
 
     zsrc[0:4, :] = win_ref[...].astype(F32)
     zsrc[4:8, :] = wout_ref[...].astype(F32)

time: 127 us -> 127 us (level)
  no operation moved by 1% of the time
where the time goes in v5:
time: 127 us
  Pallas kernels  122 us (96%)
  local copies, waits for them, and re-layouts  4.38 us (3%)
    pallas_call x1, Pallas kernels, body(): pl.pallas_call(kernel, out_shape=out_shape, in_specs=[hbm] + [vmem] * 5 +...  122 us
    squeeze x1, local copies, waits for them, and re-layouts, body(): fields[1]  3.14 us

profile of v5, /device:TPU:1, one launch (start us, length us, event | category | flops | bytes accessed | tf_op | source)
XLA Modules:
  0.0 126.7 jit_solution(7048338941799543575)
XLA Ops:
  0.6 121.6 %spectral_block.1 = (bf16[2,12,180,256]{3,2,1,0:T(8,128)(2,1)}, f32[2,4,256]{2,1,0:T(4,128)}, f32[2,2,32,32]{3,2,1,0:T(8,128)}) custom-call(bf16[12,180,256]{2,1,0:T(8,128)(2,1)} %refs_0_.1, f32[1,256]{1,0:T(1,128)} %bitcast.21, bf16[4,256]{1,0:T(4,128)(2,1)} %refs_2_.1, bf16[4,256]{1,0:T(4,128)(2,1)} %refs_3_.1, bf16[2,32,32]{2,1,0:T(8,128)(2,1)} %bitcast.19, ...), custom_call_target="tpu_custom_call" | custom-call | tf_op jit(solution)/shard_map/spectral_block/pallas_call | solution.py:680
  122.3 0.0 copy-start.1
  122.3 0.0 copy-start
  122.3 3.1 %slice_bitcast_fusion = (bf16[12,180,256]{2,1,0:T(8,128)(2,1)}, bf16[12,180,256]{2,1,0:T(8,128)(2,1)}) fusion(bf16[2,12,180,256]{3,2,1,0:T(8,128)(2,1)} %get-tuple-element.9), kind=kLoop, calls=%fused_computation | loop fusion | bytes 4423680 | tf_op jit(solution)/shard_map/squeeze | solution.py:702
  125.4 0.0 copy-done.1
  125.4 0.6 slice_bitcast_fusion.4
  126.0 0.0 copy-done
  126.0 0.6 slice_bitcast_fusion.2
Async XLA Ops:
  122.3 3.2 %copy-start.1 = (f32[2,4,256]{2,1,0:T(4,128)S(1)}, f32[2,4,256]{2,1,0:T(4,128)}, u32[]{:S(2)}) copy-start(f32[2,4,256]{2,1,0:T(4,128)} %get-tuple-element.10) | copy-start | bytes 24580
  122.3 3.8 %copy-start = (f32[2,2,32,32]{3,2,1,0:T(8,128)S(1)}, f32[2,2,32,32]{3,2,1,0:T(8,128)}, u32[]{:S(2)}) copy-start(f32[2,2,32,32]{3,2,1,0:T(8,128)} %get-tuple-element.11) | copy-start | bytes 49156
